TPU v7x, 32 devices: a whole 2x2x4 slice. The times are simulated.
32 devices in a mesh: seg: 4 (over y, core), mic: 8 (over z, x).
Axes of the slice: x: 2, y: 2, z: 4, core: 2. Of those that a mesh axis runs over, the one named last changes fastest.
Arguments:
- time_data: bfloat16 [128, 512, 1024], P('seg', 'mic'), may hold values from -6 to 6
- order_bin: int32 [1], replicated, may hold values from 32 to 203
- mic_pos: int32 [3, 512], replicated, may hold values from -2000 to 2000
- grid_pos: int32 [3, 16384], P(None, 'mic'), may hold values from -1500 to 1500
Outputs:
- beam_power: float32 [8, 2048], P('mic', 'seg')
All inputs are finite; a program needn't handle non-finite values.
Results may differ from a plain program's by a relative error of at most 0.00083.
Values may be sent and summed in bfloat16 or wider, within the bound.
No kernel may reach another device: no remote copies, remote signals or barrier semaphores. Data moves between devices by JAX's collectives and lax.ppermute only.
A program may use at most 256 MiB of HBM per device.

v0:
```python
import math

import jax
import jax.numpy as jnp
from jax import lax
from jax.sharding import PartitionSpec as P


def spectral_table(order_value, samples):
    times = jnp.arange(samples, dtype=jnp.int32)
    turned = order_value * times % samples
    angle = turned.astype(jnp.float32) * (2.0 * math.pi / samples)
    window = 0.5 - 0.5 * jnp.cos(times.astype(jnp.float32) * (2.0 * math.pi / samples))
    return jnp.stack([window * jnp.cos(angle), -(window * jnp.sin(angle))]).astype(jnp.bfloat16)


def stacked_left(spectra):
    real_part = spectra[0]
    imag_part = spectra[1]
    upper = jnp.concatenate([real_part, -imag_part], axis=1)
    lower = jnp.concatenate([imag_part, real_part], axis=1)
    return jnp.concatenate([upper, lower], axis=0)


def beam_block(left, mic_part, points, wave):
    offsets = (points[:, None, :] - mic_part[:, :, None]).astype(jnp.float32) * 0.001
    distance = jnp.sqrt(offsets[0] * offsets[0] + offsets[1] * offsets[1] + offsets[2] * offsets[2])
    phase = wave * distance
    steering = jnp.concatenate([jnp.cos(phase), jnp.sin(phase)], axis=0).astype(jnp.bfloat16)
    return jnp.dot(left, steering, preferred_element_type=jnp.float32)


def make_folder(points, mic_pos, wave):

    def accumulate(carry, piece, start):
        left = stacked_left(piece)
        return beam_block(left, mic_pos, points, wave)

    return accumulate


def shards(time_data, order_bin, mic_pos, grid_pos):
    seg_dev = time_data.shape[0]
    mic_dev = time_data.shape[1]
    samples = time_data.shape[2]
    table = spectral_table(order_bin[0], samples)
    rows = time_data.reshape(seg_dev * mic_dev, samples)
    spec = jnp.dot(rows, table.T, preferred_element_type=jnp.float32)
    spectra = spec.T.reshape(2, seg_dev, mic_dev).astype(jnp.bfloat16)
    wave = (
        order_bin[0].astype(jnp.float32)
        * jnp.float32(2.0 * math.pi * 51200.0 / 343.0)
        / jnp.float32(samples)
    )
    seg_count = lax.axis_size("seg")
    seg_total = seg_count * seg_dev
    mic_total = lax.axis_size("mic") * mic_dev
    denom = jnp.float32(seg_total * mic_total * 0.375 * samples)
    slab_width = grid_pos.shape[1]
    own_width = slab_width // seg_count
    offset = lax.axis_index("seg") * own_width
    own_points = lax.dynamic_slice_in_dim(grid_pos, offset, own_width, 1)
    every_segment = lax.all_gather(spectra, "seg", axis=1, tiled=True)
    folder = make_folder(own_points, mic_pos, wave)
    empty = jnp.zeros((2 * seg_total, own_width), jnp.float32)
    beams = folder(empty, lax.all_gather(every_segment, "mic", axis=2, tiled=True), jnp.int32(0))
    beam_power = jnp.sum(beams * beams, axis=0) / denom
    return beam_power.reshape(1, own_width)


def solution(mesh):
    placed = (P("seg", "mic", None), P(), P(), P(None, "mic"))
    return jax.shard_map(
        shards, mesh=mesh, in_specs=placed, out_specs=P("mic", "seg"), check_vma=False
    )
```

profile of v0, /device:TPU:0, one launch (start us, length us, event | category | flops | bytes accessed | tf_op | source)
XLA Modules:
  0.0 52.1 jit_solution(15302869624140353297)
XLA Ops:
  0.0 0.0 copy-start
  0.0 0.8 %copy-done = s32[3,2048]{1,0:T(4,128)S(1)} copy-done((s32[3,2048]{1,0:T(4,128)S(1)}, s32[3,2048]{1,0:T(4,128)}, u32[]{:S(2)}) %copy-start) | copy-done | bytes 24600
  0.8 1.1 %convert_multiply_fusion = f32[3,512,512]{2,1,0:T(8,128)S(1)} fusion(s32[3,512]{1,0:T(4,128)} %param.6, s32[3,512]{1,0:T(4,128)S(1)} %constant_dynamic-slice_fusion), kind=kLoop, calls=%fused_computation | loop fusion | flops 2359296 | bytes 3158016 | tf_op jit(solution)/shard_map/mul | solution.py:26
  2.5 0.0 copy-start.1
  2.5 4.5 %fusion.8 = (bf16[512,512]{1,0:T(8,128)(2,1)}, f32[1,512,512]{2,1,0:T(8,128)S(1)}) fusion(f32[3,512,512]{2,1,0:T(8,128)S(1)} %convert_multiply_fusion, f32[]{:T(128)S(6)} %div.11), kind=kLoop, calls=%fused_computation.16 | loop fusion | flops 1835008 | bytes 4718596 | tf_op jit(solution)/shard_map/convert
  7.0 3.4 %fusion.9 = bf16[512,512]{1,0:T(8,128)(2,1)S(1)} fusion(f32[1,512,512]{2,1,0:T(8,128)S(1)} %get-tuple-element.6), kind=kLoop, calls=%fused_computation.17 | loop fusion | flops 262144 | bytes 1572864 | tf_op jit(solution)/shard_map/convert.1
  10.4 0.3 negate_convert_fusion
  10.7 0.0 copy-done.1
  10.7 0.0 copy-start.2
  10.7 1.7 %convolution_convert_fusion = bf16[2,32,64]{2,0,1:T(2,128)(2,1)S(1)} fusion(bf16[32,64,1024]{2,1,0:T(8,128)(2,1)S(1)} %copy-done.1, bf16[1,1024]{1,0:T(2,128)(2,1)S(1)} %get-tuple-element.9, bf16[1,1024]{1,0:T(2,128)(2,1)S(1)} %get-tuple-element.10), kind=kOutput, calls=%fused_computation.3 | convolution fusion | flops 8400896 | bytes 4206592 | tf_op jit(solution)/shard_map/dot_general | solution.py:48
  12.4 6.2 %all_gather.6 = bf16[2,128,64]{2,0,1:T(2,128)(2,1)S(1)} all-gather(bf16[2,32,64]{2,0,1:T(2,128)(2,1)S(1)} %convolution_convert_fusion), channel_id=1, replica_groups=mesh['seg'=4,'mic'=8] {'seg'}, dimensions={1}, use_global_device_ids=true | all-gather | bytes 40960 | tf_op jit(solution)/shard_map/all_gather | solution.py:63
  18.6 0.1 copy.6
  18.7 31.7 %all_gather.7 = bf16[2,128,512]{1,0,2:T(2,128)(2,1)S(1)} all-gather(bf16[2,128,64]{1,0,2:T(2,128)(2,1)S(1)} %copy.6), channel_id=1, replica_groups=mesh['seg'=4,'mic'=8] {'mic'}, dimensions={2}, use_global_device_ids=true | all-gather | bytes 294912 | tf_op jit(solution)/shard_map/all_gather | solution.py:66
  50.4 0.4 fusion.25
  50.8 0.1 copy.10
  51.0 0.1 copy.9
  51.1 0.0 copy-done.2
  51.1 0.5 fusion
  51.6 0.6 %broadcast_multiply_fusion = f32[512]{0:T(512)} fusion(f32[512]{0:T(512)S(1)} %fusion), kind=kLoop, calls=%fused_computation.37 | loop fusion | flops 512 | bytes 4096 | tf_op jit(solution)/shard_map/div | solution.py:67
  (2 shorter events, 0.0 us)
Async XLA Ops:
  0.0 0.8 %copy-start = (s32[3,2048]{1,0:T(4,128)S(1)}, s32[3,2048]{1,0:T(4,128)}, u32[]{:S(2)}) copy-start(s32[3,2048]{1,0:T(4,128)} %param.7) | copy-start | bytes 73732
  2.5 8.2 %copy-start.1 = (bf16[32,64,1024]{2,1,0:T(8,128)(2,1)S(1)}, bf16[32,64,1024]{2,1,0:T(8,128)(2,1)}, u32[]{:S(2)}) copy-start(bf16[32,64,1024]{2,1,0:T(8,128)(2,1)} %param.4) | copy-start | bytes 12582916
  10.7 40.4 %copy-start.2 = (bf16[512,512]{1,0:T(8,128)(2,1)S(1)}, bf16[512,512]{1,0:T(8,128)(2,1)}, u32[]{:S(2)}) copy-start(bf16[512,512]{1,0:T(8,128)(2,1)} %get-tuple-element.5) | copy-start | bytes 1572868
where the time goes:
time: 52.4 us; the launch traced here: 52.1 us
  blocking collectives  37.9 us (72%)
  other arithmetic  9.86 us (19%)
  matrix products  2.17 us (4%)
  local copies, waits for them, and re-layouts  1.49 us (3%)
  between operations  0.74 us (1%)
    all_gather x1, blocking collectives, shards(): lax.all_gather(every_segment, 'mic', axis=2, tiled=True)  31.7 us
    another operation x3, other arithmetic  8.18 us
    all_gather x1, blocking collectives, shards(): every_segment = lax.all_gather(spectra, 'seg', axis=1, tiled=True)  6.19 us
    dot_general x1, matrix products, shards(): spec = jnp.dot(rows, table.T, preferred_element_type=jnp.float32)  1.72 us
    mul x1, other arithmetic, beam_block(): (points[:, None, :] - mic_part[:, :, None]).astype(jnp.float32) * 0.001  1.08 us

commit v1 on v0

v1 whole, which is shorter than its diff:
```python
import functools
import math

import jax
import jax.numpy as jnp
import numpy as np
from jax import lax
from jax.experimental import pallas as pl
from jax.experimental.pallas import tpu as pltpu
from jax.sharding import PartitionSpec as P

LANES = 128
VMEM_LIMIT = 60 * 1024 * 1024


def fitted(values, degree):
    count = degree + 1
    nodes = 0.125 + 0.125 * np.cos((2 * np.arange(count) + 1) * np.pi / (2 * count))
    return [float(c) for c in np.linalg.solve(np.vander(nodes, count, increasing=True), values(nodes))]


COS_FIT = fitted(lambda q: np.cos(2 * np.pi * np.sqrt(q)), 6)
SIN_FIT = fitted(lambda q: np.sin(2 * np.pi * np.sqrt(q)) / np.sqrt(q), 6)


def horner(coefficients, q):
    total = jnp.full_like(q, coefficients[-1])
    for c in coefficients[-2::-1]:
        total = total * q + c
    return total


def cos_sin_turns(turns):
    r = turns - jnp.round(turns)
    q = r * r
    return horner(COS_FIT, q), r * horner(SIN_FIT, q)


def spectra_kernel(order_ref, data_ref, out_ref, held, rows_ref, sems, *, chunks):
    seg, mic, samples = held.shape
    part = seg // chunks
    copies = [
        pltpu.make_async_copy(
            data_ref.at[pl.ds(k * part, part)], held.at[pl.ds(k * part, part)], sems.at[k]
        )
        for k in range(chunks)
    ]
    for copy in copies:
        copy.start()
    times = lax.broadcasted_iota(jnp.int32, (16, samples), 1)
    row = lax.broadcasted_iota(jnp.int32, (16, samples), 0)
    turned = lax.rem(order_ref[0] * times, jnp.int32(samples))
    cos_w, _ = cos_sin_turns(times.astype(jnp.float32) * (1.0 / samples))
    cos_a, sin_a = cos_sin_turns(turned.astype(jnp.float32) * (1.0 / samples))
    window = 0.5 - 0.5 * cos_w
    table = jnp.where(row == 0, window * cos_a, jnp.where(row == 1, -(window * sin_a), 0.0))
    table = table.astype(jnp.bfloat16)
    lines = seg * mic // LANES
    per = part * mic // LANES
    for k in range(chunks):
        copies[k].wait()
        block = held[pl.ds(k * part, part)].reshape(part * mic, samples)
        spec = lax.dot_general(
            table, block, (((1,), (1,)), ((), ())), preferred_element_type=jnp.float32
        )
        for j in range(per):
            line = k * per + j
            rows_ref[pl.ds(line, 1), :] = spec[0:1, j * LANES : (j + 1) * LANES]
            rows_ref[pl.ds(lines + line, 1), :] = spec[1:2, j * LANES : (j + 1) * LANES]
    out_ref[...] = rows_ref[...].astype(jnp.bfloat16)


def spectra_of(order_bin, time_data, chunks=4):
    seg, mic, samples = time_data.shape
    lines = seg * mic // LANES
    return pl.pallas_call(
        functools.partial(spectra_kernel, chunks=chunks),
        out_shape=jax.ShapeDtypeStruct((2 * lines, LANES), jnp.bfloat16),
        in_specs=[pl.BlockSpec(memory_space=pltpu.SMEM), pl.BlockSpec(memory_space=pltpu.HBM)],
        out_specs=pl.BlockSpec(memory_space=pltpu.VMEM),
        scratch_shapes=[
            pltpu.VMEM(time_data.shape, time_data.dtype),
            pltpu.VMEM((2 * lines, LANES), jnp.float32),
            pltpu.SemaphoreType.DMA((chunks,)),
        ],
        compiler_params=pltpu.CompilerParams(vmem_limit_bytes=VMEM_LIMIT),
        cost_estimate=pl.CostEstimate(
            flops=4 * time_data.size, bytes_accessed=2 * time_data.size, transcendentals=0
        ),
    )(order_bin, time_data)


def steering_kernel(order_ref, mic_ref, grid_ref, after_ref, out_ref, column, *, masks, samples, width):
    del after_ref
    own_pair = lax.shift_right_logical(lax.axis_index("mic"), 1)
    offset = pl.multiple_of(lax.axis_index("seg") * width, width)
    per_mm = order_ref[0].astype(jnp.float32) * jnp.float32(51200.0 / 343.0 / 1000.0 / samples)
    points = grid_ref[:, pl.ds(offset, width)].astype(jnp.float32)
    for k, mask in enumerate(masks):
        start = pl.multiple_of(lax.bitwise_xor(own_pair, jnp.int32(mask)) * LANES, LANES)
        mics = mic_ref[:, pl.ds(start, LANES)].astype(jnp.float32)
        mics = jnp.concatenate([mics, jnp.zeros((5, LANES), jnp.float32)], axis=0)
        column[...] = jnp.transpose(mics)

        def sixteen(i, carry, k=k):
            first = pl.multiple_of(i * 16, 16)
            mine = column[pl.ds(first, 16), :]
            square = None
            for axis in range(3):
                gap = points[axis : axis + 1, :] - mine[:, axis : axis + 1]
                square = gap * gap if square is None else square + gap * gap
            turns = square * lax.rsqrt(jnp.maximum(square, 1.0)) * per_mm
            cosine, sine = cos_sin_turns(turns)
            out_ref[k, pl.ds(first, 16), :] = cosine.astype(jnp.bfloat16)
            out_ref[k, pl.ds(LANES + first, 16), :] = sine.astype(jnp.bfloat16)
            return carry

        lax.fori_loop(0, LANES // 16, sixteen, 0)


def steering_of(order_bin, mic_pos, grid_pos, after, masks, samples, width):
    return pl.pallas_call(
        functools.partial(steering_kernel, masks=masks, samples=samples, width=width),
        out_shape=jax.ShapeDtypeStruct((len(masks), 2 * LANES, width), jnp.bfloat16),
        in_specs=[pl.BlockSpec(memory_space=pltpu.SMEM)] + [pl.BlockSpec(memory_space=pltpu.VMEM)] * 3,
        out_specs=pl.BlockSpec(memory_space=pltpu.VMEM),
        scratch_shapes=[pltpu.VMEM((LANES, 8), jnp.float32)],
        compiler_params=pltpu.CompilerParams(vmem_limit_bytes=32 * 1024 * 1024),
        cost_estimate=pl.CostEstimate(
            flops=50 * len(masks) * LANES * width, bytes_accessed=4 * len(masks) * LANES * width, transcendentals=0
        ),
    )(order_bin, mic_pos, grid_pos, after)


def left_blocks(own, other, odd):
    pairs, rows, _ = own.shape
    own = own.astype(jnp.float32).reshape(pairs * rows, LANES)
    other = other.astype(jnp.float32).reshape(pairs * rows, LANES)
    lower = jnp.where(odd, other, own)
    upper = jnp.where(odd, own, other)
    half = lax.broadcasted_iota(jnp.int32, lower.shape, 1) < LANES // 2
    even_segs = jnp.where(half, lower, pltpu.roll(upper, LANES // 2, 1))
    odd_segs = jnp.where(half, pltpu.roll(lower, LANES // 2, 1), upper)
    return [x.reshape(pairs, rows, LANES) for x in (even_segs, odd_segs)]


def power_kernel(a_ref, b_ref, c_ref, d_ref, steer_ref, before_ref, out_ref, *, scale):
    odd = lax.bitwise_and(lax.axis_index("mic"), 1) == 1
    pieces = left_blocks(a_ref[...], b_ref[...], odd) + left_blocks(c_ref[...], d_ref[...], odd)
    pairs, rows, _ = a_ref.shape
    lines = rows // 2
    beams = None
    for k in range(pairs):
        left = []
        for piece in pieces:
            x = piece[k]
            turned = jnp.concatenate([-x[lines:], x[:lines]], axis=0)
            left.append(jnp.concatenate([x, turned], axis=1))
        left = jnp.concatenate(left, axis=0).astype(jnp.bfloat16)
        term = jnp.dot(left, steer_ref[k], preferred_element_type=jnp.float32)
        beams = term if beams is None else beams + term
    power = jnp.sum((beams * beams).reshape(-1, 8, beams.shape[1]), axis=0) + before_ref[...]
    if scale is None:
        out_ref[...] = power
    else:
        out_ref[...] = jnp.sum(power, axis=0, keepdims=True) / jnp.float32(scale)


def power_of(blocks, steering, before, scale):
    width = steering.shape[2]
    shape = (8 if scale is None else 1, width)
    pairs, rows, _ = blocks[0].shape
    return pl.pallas_call(
        functools.partial(power_kernel, scale=scale),
        out_shape=jax.ShapeDtypeStruct(shape, jnp.float32),
        in_specs=[pl.BlockSpec(memory_space=pltpu.VMEM)] * 6,
        out_specs=pl.BlockSpec(memory_space=pltpu.VMEM),
        compiler_params=pltpu.CompilerParams(vmem_limit_bytes=32 * 1024 * 1024),
        cost_estimate=pl.CostEstimate(
            flops=2 * 4 * rows * steering.size, bytes_accessed=2 * steering.size, transcendentals=0
        ),
    )(*blocks, steering, before)


def shards(time_data, order_bin, mic_pos, grid_pos):
    seg_dev, mic_dev, samples = time_data.shape
    seg_count = lax.axis_size("seg")
    mic_count = lax.axis_size("mic")
    own_width = grid_pos.shape[1] // seg_count
    denom = seg_count * seg_dev * mic_count * mic_dev * 0.375 * samples

    def swap(x, mask):
        pairs = [(i, i ^ mask) for i in range(seg_count * mic_count)]
        return lax.ppermute(x, ("seg", "mic"), pairs)

    spectra = spectra_of(order_bin, time_data)
    held = spectra[None]
    masks = [0]
    bit = mic_count // 2
    while bit > 1:
        held = jnp.concatenate([held, swap(held, bit)], axis=0)
        masks += [m ^ (bit // 2) for m in masks]
        bit //= 2
    steering = steering_of(order_bin, mic_pos, grid_pos, spectra, masks, samples, own_width)
    far = 2 * mic_count
    both = swap(held, far + 1)
    beside = swap(held, 1)
    across = swap(held, far)
    blocks = [held, beside, across, both]
    twin = swap(jnp.concatenate(blocks, axis=0), mic_count)
    pairs = len(masks)
    twins = [twin[i * pairs : (i + 1) * pairs] for i in range(4)]
    half = power_of(blocks, steering, jnp.zeros((8, own_width), jnp.float32), None)
    return power_of(twins, steering, half, denom)


def solution(mesh):
    placed = (P("seg", "mic", None), P(), P(), P(None, "mic"))
    return jax.shard_map(
        shards, mesh=mesh, in_specs=placed, out_specs=P("mic", "seg"), check_vma=False
    )
```

time: 52.4 us -> 29.3 us (0.56)
  blocking collectives: 37.9 us -> 0 us
  starting transfers between devices: 0 us -> 9.57 us
  Pallas kernels: 0 us -> 9.05 us
  other arithmetic: 9.86 us -> 1.4 us
  waiting for transfers between devices: 0 us -> 6.64 us
  matrix products: 2.17 us -> 0 us
    all_gather x2 -> x0, blocking collectives: 37.9 us -> none  [the longest x1 31.7 us: shards(): lax.all_gather(every_segment, 'mic', axis=2, tiled=True)]
    ppermute x0 -> x6, starting transfers between devices: none -> 9.57 us  [swap(): return lax.ppermute(x, ('seg', 'mic'), pairs)]
    pallas_call x0 -> x4, Pallas kernels: none -> 9.05 us  [the longest x1 4.32 us: steering_of(): pl.pallas_call(functools.partial(steering_kernel, masks=masks, samples=sa...]
    another operation x3 -> x0, other arithmetic: 8.18 us -> none
    ppermute x0 -> x6, waiting for transfers between devices: none -> 6.64 us  [swap(): return lax.ppermute(x, ('seg', 'mic'), pairs)]
    dot_general x2 -> x0, matrix products: 2.17 us -> none  [the longest x1 1.72 us: shards(): spec = jnp.dot(rows, table.T, preferred_element_type=jnp.float32)]
    concatenate x0 -> x2, other arithmetic: none -> 1.4 us  [shards(): held = jnp.concatenate([held, swap(held, bit)], axis=0)]
    mul x1 -> x0, other arithmetic: 1.08 us -> none  [beam_block(): (points[:, None, :] - mic_part[:, :, None]).astype(jnp.float32) * 0.001]
  transfers between devices with their start and end apart: 0 -> 6, of which waited for: 0 -> 3; matrix products, arithmetic and copies ran while one was open for 0% -> 3% of each run, Pallas kernels for 0% -> 16%
where the time goes in v1:
time: 29.3 us; the launch traced here: 28.9 us
  starting transfers between devices  9.57 us (33%)
  Pallas kernels  9.05 us (31%)
  waiting for transfers between devices  6.64 us (23%)
  local copies, waits for them, and re-layouts  1.49 us (5%)
  other arithmetic  1.4 us (5%)
  between operations  0.76 us (3%)
    ppermute x6, starting transfers between devices, swap(): return lax.ppermute(x, ('seg', 'mic'), pairs)  9.57 us
    ppermute x6, waiting for transfers between devices, swap(): return lax.ppermute(x, ('seg', 'mic'), pairs)  6.64 us
    pallas_call x1, Pallas kernels, steering_of(): pl.pallas_call(functools.partial(steering_kernel, masks=masks, samples=sa...  4.32 us
    pallas_call x1, Pallas kernels, spectra_of(): pl.pallas_call(functools.partial(spectra_kernel, chunks=chunks), out_shap...  3.41 us
    unnamed x11, local copies, waits for them, and re-layouts  1.46 us
    concatenate x2, other arithmetic, shards(): held = jnp.concatenate([held, swap(held, bit)], axis=0)  1.4 us
    pallas_call x2, Pallas kernels, power_of(): pl.pallas_call(functools.partial(power_kernel, scale=scale), out_shape=ja...  1.32 us
  transfers between devices with their start and end apart: 6, of which 3 were waited for; matrix products, arithmetic and copies ran while one was open for 3% of the time, Pallas kernels for 16%

profile of v1, /device:TPU:0, one launch (start us, length us, event | category | flops | bytes accessed | tf_op | source)
XLA Modules:
  0.0 28.9 jit_solution(6904750952685894644)
XLA Ops:
  0.0 0.0 copy-start.1
  0.7 3.4 %shard_map.46.after_ref = bf16[32,128]{1,0:T(8,128)(2,1)} custom-call(s32[1]{0:T(128)S(6)} %copy.10.order_ref, bf16[32,64,1024]{2,1,0:T(8,128)(2,1)} %data_ref.1), custom_call_target="tpu_custom_call" | custom-call | flops 8388608 | bytes 4194304 | tf_op jit(solution)/shard_map/pallas_call | solution.py:76
  4.1 4.1 %collective-permute-start = (bf16[1,32,128]{2,1,0:T(8,128)(2,1)}, bf16[1,32,128]{2,1,0:T(8,128)(2,1)S(1)}, u32[]{:S(2)}, u32[]{:S(2)}) collective-permute-start(bf16[1,32,128]{2,1,0:T(8,128)(2,1)} %bitcast.2), channel_id=1, source_target_pairs={{0,4},{1,5},{2,6},{3,7},{4,0},{5,1},{6,2},{7,3},{8,12},{9,13},{10,... | collective-permute-start | bytes 24584 | tf_op jit(solution)/shard_map/ppermute | solution.py:194
  8.2 0.7 %constant_dynamic-update-slice_fusion.5 = bf16[16,32,128]{2,1,0:T(8,128)(2,1)S(1)} fusion(bf16[32,128]{1,0:T(8,128)(2,1)} %shard_map.46.after_ref), kind=kLoop, calls=%fused_computation.7 | loop fusion | bytes 16384
  8.9 1.1 %collective-permute-done = bf16[1,32,128]{2,1,0:T(8,128)(2,1)S(1)} collective-permute-done((bf16[1,32,128]{2,1,0:T(8,128)(2,1)}, bf16[1,32,128]{2,1,0:T(8,128)(2,1)S(1)}, u32[]{:S(2)}, u32[]{:S(2)}) %collective-permute-start) | collective-permute-done | bytes 8224 | tf_op jit(solution)/shard_map/ppermute | solution.py:194
  10.0 0.7 %pad_maximum_fusion.1 = bf16[2,32,128]{2,1,0:T(8,128)(2,1)S(1)} fusion(bf16[1,32,128]{2,1,0:T(8,128)(2,1)S(1)} %collective-permute-done, bf16[1,32,128]{2,1,0:T(8,128)(2,1)} %bitcast.3), kind=kLoop, calls=%fused_computation.1 | loop fusion | flops 8192 | bytes 32768 | tf_op jit(solution)/shard_map/concatenate | solution.py:201
  10.7 1.9 %collective-permute-start.1 = (bf16[2,32,128]{2,1,0:T(8,128)(2,1)S(1)}, bf16[2,32,128]{2,1,0:T(8,128)(2,1)S(1)}, u32[]{:S(2)}, u32[]{:S(2)}) collective-permute-start(bf16[2,32,128]{2,1,0:T(8,128)(2,1)S(1)} %pad_maximum_fusion.1), channel_id=1, source_target_pairs={{0,2},{1,3},{2,0},{3,1},{4,6},{5,7},{6,4},{7,5},{8,10},{9,11},{10,... | collective-permute-start | bytes 49160 | tf_op jit(solution)/shard_map/ppermute | solution.py:194
  12.6 1.8 %collective-permute-done.1 = bf16[2,32,128]{2,1,0:T(8,128)(2,1)S(1)} collective-permute-done((bf16[2,32,128]{2,1,0:T(8,128)(2,1)S(1)}, bf16[2,32,128]{2,1,0:T(8,128)(2,1)S(1)}, u32[]{:S(2)}, u32[]{:S(2)}) %collective-permute-start.1) | collective-permute-done | bytes 16416 | tf_op jit(solution)/shard_map/ppermute | solution.py:194
  14.5 0.7 %pad_maximum_fusion.a_ref = bf16[4,32,128]{2,1,0:T(8,128)(2,1)S(1)} fusion(bf16[2,32,128]{2,1,0:T(8,128)(2,1)S(1)} %collective-permute-done.1, bf16[1,32,128]{2,1,0:T(8,128)(2,1)S(1)} %collective-permute-done, bf16[1,32,128]{2,1,0:T(8,128)(2,1)} %bitcast.4), kind=kLoop, calls=%fused_computation | loop fusion | flops 32768 | bytes 65536 | tf_op jit(solution)/shard_map/concatenate | solution.py:201
  15.2 2.8 %collective-permute-start.4 = (bf16[4,32,128]{2,1,0:T(8,128)(2,1)S(1)}, bf16[4,32,128]{2,1,0:T(8,128)(2,1)S(1)}, u32[]{:S(2)}, u32[]{:S(2)}) collective-permute-start(bf16[4,32,128]{2,1,0:T(8,128)(2,1)S(1)} %pad_maximum_fusion.a_ref), channel_id=1, source_target_pairs={{0,17},{1,16},{2,19},{3,18},{4,21},{5,20},{6,23},{7,22},{8,25},{9,... | collective-permute-start | bytes 98312 | tf_op jit(solution)/shard_map/ppermute | solution.py:194
  17.9 0.5 %collective-permute-start.3 = (bf16[4,32,128]{2,1,0:T(8,128)(2,1)S(1)}, bf16[4,32,128]{2,1,0:T(8,128)(2,1)S(1)}, u32[]{:S(2)}, u32[]{:S(2)}) collective-permute-start(bf16[4,32,128]{2,1,0:T(8,128)(2,1)S(1)} %pad_maximum_fusion.a_ref), channel_id=1, source_target_pairs={{0,16},{1,17},{2,18},{3,19},{4,20},{5,21},{6,22},{7,23},{8,24},{9,... | collective-permute-start | bytes 98312 | tf_op jit(solution)/shard_map/ppermute | solution.py:194
  18.5 0.2 collective-permute-start.2
  18.7 3.7 %collective-permute-done.2.b_ref = bf16[4,32,128]{2,1,0:T(8,128)(2,1)S(1)} collective-permute-done((bf16[4,32,128]{2,1,0:T(8,128)(2,1)S(1)}, bf16[4,32,128]{2,1,0:T(8,128)(2,1)S(1)}, u32[]{:S(2)}, u32[]{:S(2)}) %collective-permute-start.2) | collective-permute-done | bytes 32800 | tf_op jit(solution)/shard_map/ppermute | solution.py:194
  22.4 0.0 collective-permute-done.3.c_ref
  22.4 0.0 collective-permute-done.4.d_ref
  22.4 0.1 collective-permute-start.5
  22.5 0.0 copy-done.1
  22.5 0.0 copy-done.2
  22.5 0.0 copy-start
  22.5 0.7 %copy-done = bf16[32,128]{1,0:T(8,128)(2,1)S(1)} copy-done((bf16[32,128]{1,0:T(8,128)(2,1)S(1)}, bf16[32,128]{1,0:T(8,128)(2,1)}, u32[]{:S(2)}) %copy-start) | copy-done | bytes 8216
  23.2 4.3 %shard_map.47.steer_ref = bf16[4,256,512]{2,1,0:T(8,128)(2,1)S(1)} custom-call(s32[1]{0:T(128)S(6)} %copy.10.order_ref, s32[3,512]{1,0:T(4,128)S(1)} %copy-done.2, s32[3,2048]{1,0:T(4,128)S(1)} %copy-done.1, bf16[32,128]{1,0:T(8,128)(2,1)S(1)} %copy-done), custom_call_target="tpu_custom_call" | custom-call | flops 13107200 | bytes 1048576 | tf_op jit(solution)/shard_map/pallas_call | solution.py:122
  27.6 0.4 %shard_map.48.before_ref = f32[8,512]{1,0:T(8,128)S(1)} custom-call(bf16[4,32,128]{2,1,0:T(8,128)(2,1)S(1)} %pad_maximum_fusion.a_ref, bf16[4,32,128]{2,1,0:T(8,128)(2,1)S(1)} %collective-permute-done.2.b_ref, bf16[4,32,128]{2,1,0:T(8,128)(2,1)S(1)} %collective-permute-done.3.c_ref, bf16[4,32,128]{2,1,0:T(8,128)(2,1)S(1)} %collective-permute-done.4.d_ref, ...), custom_call_target="tpu_custom_call" | custom-call | flops 134217728 | bytes 1048576 | tf_op jit(solution)/shard_map/pallas_call | solution.py:173
  27.9 0.0 collective-permute-done.5
  28.0 1.0 %shard_map.49 = f32[1,512]{1,0:T(1,128)} custom-call(bf16[4,32,128]{2,1,0:T(8,128)(2,1)S(1)} %get-tuple-element.8.a_ref, bf16[4,32,128]{2,1,0:T(8,128)(2,1)S(1)} %get-tuple-element.7.b_ref, bf16[4,32,128]{2,1,0:T(8,128)(2,1)S(1)} %get-tuple-element.6.c_ref, bf16[4,32,128]{2,1,0:T(8,128)(2,1)S(1)} %get-tuple-element.5.d_ref, ...), custom_call_target="tpu_custom_call" | custom-call | flops 134217728 | bytes 1048576 | tf_op jit(solution)/shard_map/pallas_call | solution.py:173
  (8 shorter events, 0.1 us)
Async XLA Ops:
  0.0 22.5 %copy-start.1 = (s32[3,2048]{1,0:T(4,128)S(1)}, s32[3,2048]{1,0:T(4,128)}, u32[]{:S(2)}) copy-start(s32[3,2048]{1,0:T(4,128)} %grid_ref.1) | copy-start | bytes 73732
  0.0 22.5 %copy-start.2 = (s32[3,512]{1,0:T(4,128)S(1)}, s32[3,512]{1,0:T(4,128)}, u32[]{:S(2)}) copy-start(s32[3,512]{1,0:T(4,128)} %mic_ref.1) | copy-start | bytes 18436
  4.1 5.9 %collective-permute-start = (bf16[1,32,128]{2,1,0:T(8,128)(2,1)}, bf16[1,32,128]{2,1,0:T(8,128)(2,1)S(1)}, u32[]{:S(2)}, u32[]{:S(2)}) collective-permute-start(bf16[1,32,128]{2,1,0:T(8,128)(2,1)} %bitcast.2), channel_id=1, source_target_pairs={{0,4},{1,5},{2,6},{3,7},{4,0},{5,1},{6,2},{7,3},{8,12},{9,13},{10,... | collective-permute-start | bytes 24584 | tf_op jit(solution)/shard_map/ppermute | solution.py:194
  10.7 3.7 %collective-permute-start.1 = (bf16[2,32,128]{2,1,0:T(8,128)(2,1)S(1)}, bf16[2,32,128]{2,1,0:T(8,128)(2,1)S(1)}, u32[]{:S(2)}, u32[]{:S(2)}) collective-permute-start(bf16[2,32,128]{2,1,0:T(8,128)(2,1)S(1)} %pad_maximum_fusion.1), channel_id=1, source_target_pairs={{0,2},{1,3},{2,0},{3,1},{4,6},{5,7},{6,4},{7,5},{8,10},{9,11},{10,... | collective-permute-start | bytes 49160 | tf_op jit(solution)/shard_map/ppermute | solution.py:194
  15.2 7.2 %collective-permute-start.4 = (bf16[4,32,128]{2,1,0:T(8,128)(2,1)S(1)}, bf16[4,32,128]{2,1,0:T(8,128)(2,1)S(1)}, u32[]{:S(2)}, u32[]{:S(2)}) collective-permute-start(bf16[4,32,128]{2,1,0:T(8,128)(2,1)S(1)} %pad_maximum_fusion.a_ref), channel_id=1, source_target_pairs={{0,17},{1,16},{2,19},{3,18},{4,21},{5,20},{6,23},{7,22},{8,25},{9,... | collective-permute-start | bytes 98312 | tf_op jit(solution)/shard_map/ppermute | solution.py:194
  17.9 4.4 %collective-permute-start.3 = (bf16[4,32,128]{2,1,0:T(8,128)(2,1)S(1)}, bf16[4,32,128]{2,1,0:T(8,128)(2,1)S(1)}, u32[]{:S(2)}, u32[]{:S(2)}) collective-permute-start(bf16[4,32,128]{2,1,0:T(8,128)(2,1)S(1)} %pad_maximum_fusion.a_ref), channel_id=1, source_target_pairs={{0,16},{1,17},{2,18},{3,19},{4,20},{5,21},{6,22},{7,23},{8,24},{9,... | collective-permute-start | bytes 98312 | tf_op jit(solution)/shard_map/ppermute | solution.py:194
  18.5 3.9 %collective-permute-start.2 = (bf16[4,32,128]{2,1,0:T(8,128)(2,1)S(1)}, bf16[4,32,128]{2,1,0:T(8,128)(2,1)S(1)}, u32[]{:S(2)}, u32[]{:S(2)}) collective-permute-start(bf16[4,32,128]{2,1,0:T(8,128)(2,1)S(1)} %pad_maximum_fusion.a_ref), channel_id=1, source_target_pairs={{0,1},{1,0},{2,3},{3,2},{4,5},{5,4},{6,7},{7,6},{8,9},{9,8},{10,11... | collective-permute-start | bytes 98312 | tf_op jit(solution)/shard_map/ppermute | solution.py:194
  22.4 5.5 %collective-permute-start.5 = (bf16[16,32,128]{2,1,0:T(8,128)(2,1)S(1)}, bf16[16,32,128]{2,1,0:T(8,128)(2,1)S(1)}, u32[]{:S(2)}, u32[]{:S(2)}) collective-permute-start(bf16[16,32,128]{2,1,0:T(8,128)(2,1)S(1)} %constant_dynamic-update-slice_fusion), channel_id=1, source_target_pairs={{0,8},{1,9},{2,10},{3,11},{4,12},{5,13},{6,14},{7,15},{8,0},{9,1},... | collective-permute-start | bytes 393224 | tf_op jit(solution)/shard_map/ppermute | solution.py:194
  22.5 0.7 %copy-start = (bf16[32,128]{1,0:T(8,128)(2,1)S(1)}, bf16[32,128]{1,0:T(8,128)(2,1)}, u32[]{:S(2)}) copy-start(bf16[32,128]{1,0:T(8,128)(2,1)} %shard_map.46.after_ref) | copy-start | bytes 24580

commit v2 on v1

--- a/solution.py
+++ b/solution.py
@@ -10,7 +10,8 @@
 from jax.sharding import PartitionSpec as P
 
 LANES = 128
-VMEM_LIMIT = 60 * 1024 * 1024
+MIB = 1024 * 1024
+NEAREST = 1.5 * 2.0**23
 
 
 def fitted(values, degree):
@@ -20,82 +21,91 @@
 
 
 COS_FIT = fitted(lambda q: np.cos(2 * np.pi * np.sqrt(q)), 6)
-SIN_FIT = fitted(lambda q: np.sin(2 * np.pi * np.sqrt(q)) / np.sqrt(q), 6)
+SIN_FIT = fitted(lambda q: np.sin(2 * np.pi * np.sqrt(q)) / np.sqrt(q), 5)
 
 
 def horner(coefficients, q):
-    total = jnp.full_like(q, coefficients[-1])
-    for c in coefficients[-2::-1]:
+    total = q * coefficients[-1] + coefficients[-2]
+    for c in coefficients[-3::-1]:
         total = total * q + c
     return total
 
 
 def cos_sin_turns(turns):
-    r = turns - jnp.round(turns)
+    r = turns - ((turns + NEAREST) - NEAREST)
     q = r * r
     return horner(COS_FIT, q), r * horner(SIN_FIT, q)
 
 
-def spectra_kernel(order_ref, data_ref, out_ref, held, rows_ref, sems, *, chunks):
+def spectra_kernel(order_ref, data_ref, out_ref, scale_ref, held, rows_ref, order_s, sems, order_sem, *, parts):
     seg, mic, samples = held.shape
-    part = seg // chunks
+    starts = [sum(parts[:k]) for k in range(len(parts))]
     copies = [
-        pltpu.make_async_copy(
-            data_ref.at[pl.ds(k * part, part)], held.at[pl.ds(k * part, part)], sems.at[k]
-        )
-        for k in range(chunks)
+        pltpu.make_async_copy(data_ref.at[pl.ds(a, n)], held.at[pl.ds(a, n)], sems.at[k])
+        for k, (a, n) in enumerate(zip(starts, parts))
     ]
+    order_copy = pltpu.make_async_copy(order_ref, order_s, order_sem)
+    order_copy.start()
     for copy in copies:
         copy.start()
-    times = lax.broadcasted_iota(jnp.int32, (16, samples), 1)
-    row = lax.broadcasted_iota(jnp.int32, (16, samples), 0)
-    turned = lax.rem(order_ref[0] * times, jnp.int32(samples))
+    times = lax.broadcasted_iota(jnp.int32, (8, samples), 1)
+    row = lax.broadcasted_iota(jnp.int32, (8, samples), 0)
     cos_w, _ = cos_sin_turns(times.astype(jnp.float32) * (1.0 / samples))
+    window = 0.5 - 0.5 * cos_w
+    order_copy.wait()
+    order = order_s[0]
+    per_mm = order.astype(jnp.float32) * jnp.float32(51200.0 / 343.0 / 1000.0 / samples)
+    scale_ref[...] = jnp.full(scale_ref.shape, per_mm)
+    turned = lax.rem(order * times, jnp.int32(samples))
     cos_a, sin_a = cos_sin_turns(turned.astype(jnp.float32) * (1.0 / samples))
-    window = 0.5 - 0.5 * cos_w
     table = jnp.where(row == 0, window * cos_a, jnp.where(row == 1, -(window * sin_a), 0.0))
     table = table.astype(jnp.bfloat16)
     lines = seg * mic // LANES
-    per = part * mic // LANES
-    for k in range(chunks):
+    found = []
+    for k, (a, n) in enumerate(zip(starts, parts)):
         copies[k].wait()
-        block = held[pl.ds(k * part, part)].reshape(part * mic, samples)
+        block = held[pl.ds(a, n)].reshape(n * mic, samples)
         spec = lax.dot_general(
             table, block, (((1,), (1,)), ((), ())), preferred_element_type=jnp.float32
         )
-        for j in range(per):
-            line = k * per + j
-            rows_ref[pl.ds(line, 1), :] = spec[0:1, j * LANES : (j + 1) * LANES]
-            rows_ref[pl.ds(lines + line, 1), :] = spec[1:2, j * LANES : (j + 1) * LANES]
+        found += [spec[:, j : j + LANES] for j in range(0, n * mic, LANES)]
+    for line, spec in enumerate(found):
+        rows_ref[pl.ds(line, 1), :] = spec[0:1]
+        rows_ref[pl.ds(lines + line, 1), :] = spec[1:2]
     out_ref[...] = rows_ref[...].astype(jnp.bfloat16)
 
 
-def spectra_of(order_bin, time_data, chunks=4):
+def spectra_of(order_bin, time_data):
     seg, mic, samples = time_data.shape
     lines = seg * mic // LANES
+    parts = (seg // 2, seg // 2)
     return pl.pallas_call(
-        functools.partial(spectra_kernel, chunks=chunks),
-        out_shape=jax.ShapeDtypeStruct((2 * lines, LANES), jnp.bfloat16),
-        in_specs=[pl.BlockSpec(memory_space=pltpu.SMEM), pl.BlockSpec(memory_space=pltpu.HBM)],
-        out_specs=pl.BlockSpec(memory_space=pltpu.VMEM),
+        functools.partial(spectra_kernel, parts=parts),
+        out_shape=[
+            jax.ShapeDtypeStruct((2 * lines, LANES), jnp.bfloat16),
+            jax.ShapeDtypeStruct((8, LANES), jnp.float32),
+        ],
+        in_specs=[pl.BlockSpec(memory_space=pltpu.HBM)] * 2,
+        out_specs=[pl.BlockSpec(memory_space=pltpu.VMEM)] * 2,
         scratch_shapes=[
             pltpu.VMEM(time_data.shape, time_data.dtype),
             pltpu.VMEM((2 * lines, LANES), jnp.float32),
-            pltpu.SemaphoreType.DMA((chunks,)),
+            pltpu.SMEM((1,), jnp.int32),
+            pltpu.SemaphoreType.DMA((len(parts),)),
+            pltpu.SemaphoreType.DMA,
         ],
-        compiler_params=pltpu.CompilerParams(vmem_limit_bytes=VMEM_LIMIT),
+        compiler_params=pltpu.CompilerParams(vmem_limit_bytes=51 * MIB),
         cost_estimate=pl.CostEstimate(
             flops=4 * time_data.size, bytes_accessed=2 * time_data.size, transcendentals=0
         ),
     )(order_bin, time_data)
 
 
-def steering_kernel(order_ref, mic_ref, grid_ref, after_ref, out_ref, column, *, masks, samples, width):
-    del after_ref
+def steering_kernel(scale_ref, mic_ref, grid_ref, out_ref, column, *, masks, width):
     own_pair = lax.shift_right_logical(lax.axis_index("mic"), 1)
     offset = pl.multiple_of(lax.axis_index("seg") * width, width)
-    per_mm = order_ref[0].astype(jnp.float32) * jnp.float32(51200.0 / 343.0 / 1000.0 / samples)
     points = grid_ref[:, pl.ds(offset, width)].astype(jnp.float32)
+    per_mm = scale_ref[0:1, 0:1]
     for k, mask in enumerate(masks):
         start = pl.multiple_of(lax.bitwise_xor(own_pair, jnp.int32(mask)) * LANES, LANES)
         mics = mic_ref[:, pl.ds(start, LANES)].astype(jnp.float32)
@@ -115,21 +125,21 @@
             out_ref[k, pl.ds(LANES + first, 16), :] = sine.astype(jnp.bfloat16)
             return carry
 
-        lax.fori_loop(0, LANES // 16, sixteen, 0)
-
-
-def steering_of(order_bin, mic_pos, grid_pos, after, masks, samples, width):
+        lax.fori_loop(0, LANES // 16, sixteen, 0, unroll=LANES // 16)
+
+
+def steering_of(scale, mic_pos, grid_pos, masks, width):
     return pl.pallas_call(
-        functools.partial(steering_kernel, masks=masks, samples=samples, width=width),
+        functools.partial(steering_kernel, masks=masks, width=width),
         out_shape=jax.ShapeDtypeStruct((len(masks), 2 * LANES, width), jnp.bfloat16),
-        in_specs=[pl.BlockSpec(memory_space=pltpu.SMEM)] + [pl.BlockSpec(memory_space=pltpu.VMEM)] * 3,
+        in_specs=[pl.BlockSpec(memory_space=pltpu.VMEM)] * 3,
         out_specs=pl.BlockSpec(memory_space=pltpu.VMEM),
         scratch_shapes=[pltpu.VMEM((LANES, 8), jnp.float32)],
-        compiler_params=pltpu.CompilerParams(vmem_limit_bytes=32 * 1024 * 1024),
+        compiler_params=pltpu.CompilerParams(vmem_limit_bytes=32 * MIB),
         cost_estimate=pl.CostEstimate(
             flops=50 * len(masks) * LANES * width, bytes_accessed=4 * len(masks) * LANES * width, transcendentals=0
         ),
-    )(order_bin, mic_pos, grid_pos, after)
+    )(scale, mic_pos, grid_pos)
 
 
 def left_blocks(own, other, odd):
@@ -175,7 +185,7 @@
         out_shape=jax.ShapeDtypeStruct(shape, jnp.float32),
         in_specs=[pl.BlockSpec(memory_space=pltpu.VMEM)] * 6,
         out_specs=pl.BlockSpec(memory_space=pltpu.VMEM),
-        compiler_params=pltpu.CompilerParams(vmem_limit_bytes=32 * 1024 * 1024),
+        compiler_params=pltpu.CompilerParams(vmem_limit_bytes=32 * MIB),
         cost_estimate=pl.CostEstimate(
             flops=2 * 4 * rows * steering.size, bytes_accessed=2 * steering.size, transcendentals=0
         ),
@@ -193,15 +203,21 @@
         pairs = [(i, i ^ mask) for i in range(seg_count * mic_count)]
         return lax.ppermute(x, ("seg", "mic"), pairs)
 
-    spectra = spectra_of(order_bin, time_data)
-    held = spectra[None]
+    spectra, scale = spectra_of(order_bin, time_data)
     masks = [0]
     bit = mic_count // 2
     while bit > 1:
-        held = jnp.concatenate([held, swap(held, bit)], axis=0)
         masks += [m ^ (bit // 2) for m in masks]
         bit //= 2
-    steering = steering_of(order_bin, mic_pos, grid_pos, spectra, masks, samples, own_width)
+    steering = steering_of(scale, mic_pos, grid_pos, masks, own_width)
+    held = spectra[None]
+    bit = mic_count // 2
+    while bit > 1:
+        came = swap(held, bit)
+        if bit == mic_count // 2:
+            came, steering = lax.optimization_barrier((came, steering))
+        held = jnp.concatenate([held, came], axis=0)
+        bit //= 2
     far = 2 * mic_count
     both = swap(held, far + 1)
     beside = swap(held, 1)

time: 29.3 us -> 22.9 us (0.78)
  Pallas kernels: 9.05 us -> 5.88 us
  local copies, waits for them, and re-layouts: 1.49 us -> 0.07 us
  other arithmetic: 1.4 us -> 0.01 us
    pallas_call x2, Pallas kernels: 7.73 us -> 4.57 us  [the longest x1 2.94 us: spectra_of(): pl.pallas_call(functools.partial(spectra_kernel, parts=parts), out_shape=...]
    unnamed x11 -> x9, local copies, waits for them, and re-layouts: 1.46 us -> 0.04 us
    concatenate x2, other arithmetic: 1.4 us -> 0.01 us  [shards(): held = jnp.concatenate([held, came], axis=0)]
  transfers between devices with their start and end apart: 6 -> 6, of which waited for: 3 -> 3; matrix products, arithmetic and copies ran while one was open for 3% -> 0% of each run, Pallas kernels for 16% -> 9%
where the time goes in v2:
time: 22.9 us; the launch traced here: 22.7 us
  starting transfers between devices  9.53 us (42%)
  waiting for transfers between devices  6.49 us (28%)
  Pallas kernels  5.88 us (26%)
  between operations  0.74 us (3%)
    ppermute x6, starting transfers between devices, swap(): return lax.ppermute(x, ('seg', 'mic'), pairs)  9.53 us
    ppermute x6, waiting for transfers between devices, swap(): return lax.ppermute(x, ('seg', 'mic'), pairs)  6.49 us
    pallas_call x1, Pallas kernels, spectra_of(): pl.pallas_call(functools.partial(spectra_kernel, parts=parts), out_shape=...  2.94 us
    pallas_call x1, Pallas kernels, steering_of(): pl.pallas_call(functools.partial(steering_kernel, masks=masks, width=widt...  1.63 us
    pallas_call x2, Pallas kernels, power_of(): pl.pallas_call(functools.partial(power_kernel, scale=scale), out_shape=ja...  1.31 us
  transfers between devices with their start and end apart: 6, of which 3 were waited for; matrix products, arithmetic and copies ran while one was open for 0% of the time, Pallas kernels for 9%

profile of v2, /device:TPU:0, one launch (start us, length us, event | category | flops | bytes accessed | tf_op | source)
XLA Modules:
  0.0 22.7 jit_solution(2996688018476439023)
XLA Ops:
  0.0 0.0 copy-start
  0.0 0.0 copy-start.1
  0.7 2.9 %shard_map.46 = (bf16[32,128]{1,0:T(8,128)(2,1)S(1)}, f32[8,128]{1,0:T(8,128)S(1)}) custom-call(s32[1]{0:T(128)S(6)} %copy.10.order_ref, bf16[32,64,1024]{2,1,0:T(8,128)(2,1)} %data_ref.1), custom_call_target="tpu_custom_call" | custom-call | flops 8388608 | bytes 4194304 | tf_op jit(solution)/shard_map/pallas_call | solution.py:82
  3.6 4.1 %collective-permute-start = (bf16[1,32,128]{2,1,0:T(8,128)(2,1)S(1)}, bf16[1,32,128]{2,1,0:T(8,128)(2,1)S(1)}, u32[]{:S(2)}, u32[]{:S(2)}) collective-permute-start(bf16[1,32,128]{2,1,0:T(8,128)(2,1)S(1)} %bitcast.2), channel_id=1, source_target_pairs={{0,4},{1,5},{2,6},{3,7},{4,0},{5,1},{6,2},{7,3},{8,12},{9,13},{10,... | collective-permute-start | bytes 24584 | tf_op jit(solution)/shard_map/ppermute | solution.py:204
  7.7 0.0 copy-done
  7.7 0.0 copy-done.1
  7.7 1.6 %shard_map.47.steer_ref = bf16[4,256,512]{2,1,0:T(8,128)(2,1)S(1)} custom-call(f32[8,128]{1,0:T(8,128)S(1)} %get-tuple-element.10.scale_ref, s32[3,512]{1,0:T(4,128)S(1)} %copy-done.1, s32[3,2048]{1,0:T(4,128)S(1)} %copy-done), custom_call_target="tpu_custom_call" | custom-call | flops 13107200 | bytes 1048576 | tf_op jit(solution)/shard_map/pallas_call | solution.py:132
  9.4 0.0 collective-permute-done
  9.4 1.9 %collective-permute-start.1 = (bf16[2,32,128]{2,1,0:T(8,128)(2,1)S(1)}, bf16[2,32,128]{2,1,0:T(8,128)(2,1)S(1)}, u32[]{:S(2)}, u32[]{:S(2)}) collective-permute-start(bf16[2,32,128]{2,1,0:T(8,128)(2,1)S(1)} %pad_maximum_fusion.1), channel_id=1, source_target_pairs={{0,2},{1,3},{2,0},{3,1},{4,6},{5,7},{6,4},{7,5},{8,10},{9,11},{10,... | collective-permute-start | bytes 49160 | tf_op jit(solution)/shard_map/ppermute | solution.py:204
  11.3 1.9 %collective-permute-done.1 = bf16[2,32,128]{2,1,0:T(8,128)(2,1)S(1)} collective-permute-done((bf16[2,32,128]{2,1,0:T(8,128)(2,1)S(1)}, bf16[2,32,128]{2,1,0:T(8,128)(2,1)S(1)}, u32[]{:S(2)}, u32[]{:S(2)}) %collective-permute-start.1) | collective-permute-done | bytes 16416 | tf_op jit(solution)/shard_map/ppermute | solution.py:204
  13.2 2.7 %collective-permute-start.4 = (bf16[4,32,128]{2,1,0:T(8,128)(2,1)S(1)}, bf16[4,32,128]{2,1,0:T(8,128)(2,1)S(1)}, u32[]{:S(2)}, u32[]{:S(2)}) collective-permute-start(bf16[4,32,128]{2,1,0:T(8,128)(2,1)S(1)} %pad_maximum_fusion.a_ref), channel_id=1, source_target_pairs={{0,17},{1,16},{2,19},{3,18},{4,21},{5,20},{6,23},{7,22},{8,25},{9,... | collective-permute-start | bytes 98312 | tf_op jit(solution)/shard_map/ppermute | solution.py:204
  15.9 0.5 %collective-permute-start.3 = (bf16[4,32,128]{2,1,0:T(8,128)(2,1)S(1)}, bf16[4,32,128]{2,1,0:T(8,128)(2,1)S(1)}, u32[]{:S(2)}, u32[]{:S(2)}) collective-permute-start(bf16[4,32,128]{2,1,0:T(8,128)(2,1)S(1)} %pad_maximum_fusion.a_ref), channel_id=1, source_target_pairs={{0,16},{1,17},{2,18},{3,19},{4,20},{5,21},{6,22},{7,23},{8,24},{9,... | collective-permute-start | bytes 98312 | tf_op jit(solution)/shard_map/ppermute | solution.py:204
  16.4 0.3 %collective-permute-start.2 = (bf16[4,32,128]{2,1,0:T(8,128)(2,1)S(1)}, bf16[4,32,128]{2,1,0:T(8,128)(2,1)S(1)}, u32[]{:S(2)}, u32[]{:S(2)}) collective-permute-start(bf16[4,32,128]{2,1,0:T(8,128)(2,1)S(1)} %pad_maximum_fusion.a_ref), channel_id=1, source_target_pairs={{0,1},{1,0},{2,3},{3,2},{4,5},{5,4},{6,7},{7,6},{8,9},{9,8},{10,11... | collective-permute-start | bytes 98312 | tf_op jit(solution)/shard_map/ppermute | solution.py:204
  16.7 3.6 %collective-permute-done.2.b_ref = bf16[4,32,128]{2,1,0:T(8,128)(2,1)S(1)} collective-permute-done((bf16[4,32,128]{2,1,0:T(8,128)(2,1)S(1)}, bf16[4,32,128]{2,1,0:T(8,128)(2,1)S(1)}, u32[]{:S(2)}, u32[]{:S(2)}) %collective-permute-start.2) | collective-permute-done | bytes 32800 | tf_op jit(solution)/shard_map/ppermute | solution.py:204
  20.3 0.0 collective-permute-done.3.c_ref
  20.3 0.0 collective-permute-done.4.d_ref
  20.3 0.1 collective-permute-start.5
  20.4 0.4 %shard_map.48.before_ref = f32[8,512]{1,0:T(8,128)S(1)} custom-call(bf16[4,32,128]{2,1,0:T(8,128)(2,1)S(1)} %pad_maximum_fusion.a_ref, bf16[4,32,128]{2,1,0:T(8,128)(2,1)S(1)} %collective-permute-done.2.b_ref, bf16[4,32,128]{2,1,0:T(8,128)(2,1)S(1)} %collective-permute-done.3.c_ref, bf16[4,32,128]{2,1,0:T(8,128)(2,1)S(1)} %collective-permute-done.4.d_ref, ...), custom_call_target="tpu_custom_call" | custom-call | flops 134217728 | bytes 1048576 | tf_op jit(solution)/shard_map/pallas_call | solution.py:183
  20.8 1.0 %collective-permute-done.5 = bf16[16,32,128]{2,1,0:T(8,128)(2,1)S(1)} collective-permute-done((bf16[16,32,128]{2,1,0:T(8,128)(2,1)S(1)}, bf16[16,32,128]{2,1,0:T(8,128)(2,1)S(1)}, u32[]{:S(2)}, u32[]{:S(2)}) %collective-permute-start.5) | collective-permute-done | bytes 131104 | tf_op jit(solution)/shard_map/ppermute | solution.py:204
  21.8 1.0 %shard_map.49 = f32[1,512]{1,0:T(1,128)} custom-call(bf16[4,32,128]{2,1,0:T(8,128)(2,1)S(1)} %get-tuple-element.16.a_ref, bf16[4,32,128]{2,1,0:T(8,128)(2,1)S(1)} %get-tuple-element.15.b_ref, bf16[4,32,128]{2,1,0:T(8,128)(2,1)S(1)} %get-tuple-element.14.c_ref, bf16[4,32,128]{2,1,0:T(8,128)(2,1)S(1)} %get-tuple-element.13.d_ref, ...), custom_call_target="tpu_custom_call" | custom-call | flops 134217728 | bytes 1048576 | tf_op jit(solution)/shard_map/pallas_call | solution.py:183
  (10 shorter events, 0.1 us)
Async XLA Ops:
  0.0 7.7 %copy-start = (s32[3,2048]{1,0:T(4,128)S(1)}, s32[3,2048]{1,0:T(4,128)}, u32[]{:S(2)}) copy-start(s32[3,2048]{1,0:T(4,128)} %grid_ref.1) | copy-start | bytes 73732
  0.0 7.7 %copy-start.1 = (s32[3,512]{1,0:T(4,128)S(1)}, s32[3,512]{1,0:T(4,128)}, u32[]{:S(2)}) copy-start(s32[3,512]{1,0:T(4,128)} %mic_ref.1) | copy-start | bytes 18436
  3.6 5.8 %collective-permute-start = (bf16[1,32,128]{2,1,0:T(8,128)(2,1)S(1)}, bf16[1,32,128]{2,1,0:T(8,128)(2,1)S(1)}, u32[]{:S(2)}, u32[]{:S(2)}) collective-permute-start(bf16[1,32,128]{2,1,0:T(8,128)(2,1)S(1)} %bitcast.2), channel_id=1, source_target_pairs={{0,4},{1,5},{2,6},{3,7},{4,0},{5,1},{6,2},{7,3},{8,12},{9,13},{10,... | collective-permute-start | bytes 24584 | tf_op jit(solution)/shard_map/ppermute | solution.py:204
  9.4 3.8 %collective-permute-start.1 = (bf16[2,32,128]{2,1,0:T(8,128)(2,1)S(1)}, bf16[2,32,128]{2,1,0:T(8,128)(2,1)S(1)}, u32[]{:S(2)}, u32[]{:S(2)}) collective-permute-start(bf16[2,32,128]{2,1,0:T(8,128)(2,1)S(1)} %pad_maximum_fusion.1), channel_id=1, source_target_pairs={{0,2},{1,3},{2,0},{3,1},{4,6},{5,7},{6,4},{7,5},{8,10},{9,11},{10,... | collective-permute-start | bytes 49160 | tf_op jit(solution)/shard_map/ppermute | solution.py:204
  13.2 7.1 %collective-permute-start.4 = (bf16[4,32,128]{2,1,0:T(8,128)(2,1)S(1)}, bf16[4,32,128]{2,1,0:T(8,128)(2,1)S(1)}, u32[]{:S(2)}, u32[]{:S(2)}) collective-permute-start(bf16[4,32,128]{2,1,0:T(8,128)(2,1)S(1)} %pad_maximum_fusion.a_ref), channel_id=1, source_target_pairs={{0,17},{1,16},{2,19},{3,18},{4,21},{5,20},{6,23},{7,22},{8,25},{9,... | collective-permute-start | bytes 98312 | tf_op jit(solution)/shard_map/ppermute | solution.py:204
  15.9 4.4 %collective-permute-start.3 = (bf16[4,32,128]{2,1,0:T(8,128)(2,1)S(1)}, bf16[4,32,128]{2,1,0:T(8,128)(2,1)S(1)}, u32[]{:S(2)}, u32[]{:S(2)}) collective-permute-start(bf16[4,32,128]{2,1,0:T(8,128)(2,1)S(1)} %pad_maximum_fusion.a_ref), channel_id=1, source_target_pairs={{0,16},{1,17},{2,18},{3,19},{4,20},{5,21},{6,22},{7,23},{8,24},{9,... | collective-permute-start | bytes 98312 | tf_op jit(solution)/shard_map/ppermute | solution.py:204
  16.4 3.9 %collective-permute-start.2 = (bf16[4,32,128]{2,1,0:T(8,128)(2,1)S(1)}, bf16[4,32,128]{2,1,0:T(8,128)(2,1)S(1)}, u32[]{:S(2)}, u32[]{:S(2)}) collective-permute-start(bf16[4,32,128]{2,1,0:T(8,128)(2,1)S(1)} %pad_maximum_fusion.a_ref), channel_id=1, source_target_pairs={{0,1},{1,0},{2,3},{3,2},{4,5},{5,4},{6,7},{7,6},{8,9},{9,8},{10,11... | collective-permute-start | bytes 98312 | tf_op jit(solution)/shard_map/ppermute | solution.py:204
  20.3 1.4 %collective-permute-start.5 = (bf16[16,32,128]{2,1,0:T(8,128)(2,1)S(1)}, bf16[16,32,128]{2,1,0:T(8,128)(2,1)S(1)}, u32[]{:S(2)}, u32[]{:S(2)}) collective-permute-start(bf16[16,32,128]{2,1,0:T(8,128)(2,1)S(1)} %constant_dynamic-update-slice_fusion), channel_id=1, source_target_pairs={{0,8},{1,9},{2,10},{3,11},{4,12},{5,13},{6,14},{7,15},{8,0},{9,1},... | collective-permute-start | bytes 393224 | tf_op jit(solution)/shard_map/ppermute | solution.py:204

commit v3 on v0

v3 whole, which is shorter than its diff:
```python
import functools
import math

import jax
import jax.numpy as jnp
import numpy as np
from jax import lax
from jax.experimental import pallas as pl
from jax.experimental.pallas import tpu as pltpu
from jax.sharding import PartitionSpec as P

LANES = 128
MIB = 1024 * 1024
NEAREST = 1.5 * 2.0**23


def fitted(values, degree):
    count = degree + 1
    nodes = 0.125 + 0.125 * np.cos((2 * np.arange(count) + 1) * np.pi / (2 * count))
    return [float(c) for c in np.linalg.solve(np.vander(nodes, count, increasing=True), values(nodes))]


COS_FIT = fitted(lambda q: np.cos(2 * np.pi * np.sqrt(q)), 6)
SIN_FIT = fitted(lambda q: np.sin(2 * np.pi * np.sqrt(q)) / np.sqrt(q), 5)


def horner(coefficients, q):
    total = q * coefficients[-1] + coefficients[-2]
    for c in coefficients[-3::-1]:
        total = total * q + c
    return total


def cos_sin_turns(turns):
    r = turns - ((turns + NEAREST) - NEAREST)
    q = r * r
    return horner(COS_FIT, q), r * horner(SIN_FIT, q)


def in_hbm(x):
    return pltpu.with_memory_space_constraint(x, pltpu.HBM)


def window_kernel(out_ref):
    times = lax.broadcasted_iota(jnp.int32, out_ref.shape, 1)
    cos_w, _ = cos_sin_turns(times.astype(jnp.float32) * (1.0 / out_ref.shape[1]))
    out_ref[...] = 0.5 - 0.5 * cos_w


def window_of(samples):
    return pl.pallas_call(
        window_kernel,
        out_shape=jax.ShapeDtypeStruct((8, samples), jnp.float32),
        out_specs=pl.BlockSpec(memory_space=pltpu.VMEM),
        compiler_params=pltpu.CompilerParams(vmem_limit_bytes=16 * MIB),
        cost_estimate=pl.CostEstimate(flops=8 * 2**30, bytes_accessed=2**24, transcendentals=0),
    )()


def table_of(order, window):
    samples = window.shape[1]
    times = lax.broadcasted_iota(jnp.int32, window.shape, 1)
    row = lax.broadcasted_iota(jnp.int32, window.shape, 0)
    turned = lax.rem(order * times, jnp.int32(samples))
    cos_a, sin_a = cos_sin_turns(turned.astype(jnp.float32) * (1.0 / samples))
    table = jnp.where(row == 0, window * cos_a, jnp.where(row == 1, -(window * sin_a), 0.0))
    return table.astype(jnp.bfloat16)


def steer(order, samples, points, mic_ref, steer_ref, column, first_pair):
    per_mm = order.astype(jnp.float32) * jnp.float32(51200.0 / 343.0 / 1000.0 / samples)
    for k in range(steer_ref.shape[0]):
        pair = first_pair + k
        mics = mic_ref[:, pair * LANES : (pair + 1) * LANES].astype(jnp.float32)
        mics = jnp.concatenate([mics, jnp.zeros((5, LANES), jnp.float32)], axis=0)
        column[...] = jnp.transpose(mics)

        def sixteen(i, carry, k=k):
            first = pl.multiple_of(i * 16, 16)
            mine = column[pl.ds(first, 16), :]
            square = None
            for axis in range(3):
                gap = points[axis : axis + 1, :] - mine[:, axis : axis + 1]
                square = gap * gap if square is None else square + gap * gap
            turns = square * lax.rsqrt(jnp.maximum(square, 1.0)) * per_mm
            cosine, sine = cos_sin_turns(turns)
            steer_ref[k, pl.ds(first, 16), :] = cosine.astype(jnp.bfloat16)
            steer_ref[k, pl.ds(LANES + first, 16), :] = sine.astype(jnp.bfloat16)
            return carry

        lax.fori_loop(0, LANES // 16, sixteen, 0, unroll=LANES // 16)


def own_points(grid_ref, width):
    offset = pl.multiple_of(lax.axis_index(("row", "core")) * width, width)
    return grid_ref[:, pl.ds(offset, width)].astype(jnp.float32)


def setup_kernel(order_ref, window_ref, mic_ref, grid_ref, table_ref, steer_ref, column, *, width):
    table_ref[...] = table_of(order_ref[0], window_ref[...])
    samples = table_ref.shape[1]
    steer(order_ref[0], samples, own_points(grid_ref, width), mic_ref, steer_ref, column, 0)


def setup_of(order_bin, window, mic_pos, grid_pos, pairs, width):
    samples = window.shape[1]
    return pl.pallas_call(
        functools.partial(setup_kernel, width=width),
        out_shape=[
            jax.ShapeDtypeStruct((8, samples), jnp.bfloat16),
            jax.ShapeDtypeStruct((pairs, 2 * LANES, width), jnp.bfloat16),
        ],
        in_specs=[pl.BlockSpec(memory_space=pltpu.SMEM)] + [pl.BlockSpec(memory_space=pltpu.VMEM)] * 3,
        out_specs=[pl.BlockSpec(memory_space=pltpu.VMEM)] * 2,
        scratch_shapes=[pltpu.VMEM((LANES, 8), jnp.float32)],
        compiler_params=pltpu.CompilerParams(vmem_limit_bytes=16 * MIB),
        cost_estimate=pl.CostEstimate(flops=2 * 2**30, bytes_accessed=2**22, transcendentals=0),
    )(order_bin, window, mic_pos, grid_pos)


def spectra_kernel(table_ref, data_ref, out_ref, rows_ref):
    seg, mic, samples = data_ref.shape
    lines = seg * mic // LANES
    block = data_ref[...].reshape(seg * mic, samples)
    spec = lax.dot_general(
        table_ref[...], block, (((1,), (1,)), ((), ())), preferred_element_type=jnp.float32
    )
    for line in range(lines):
        rows_ref[pl.ds(line, 1), :] = spec[0:1, line * LANES : (line + 1) * LANES]
        rows_ref[pl.ds(lines + line, 1), :] = spec[1:2, line * LANES : (line + 1) * LANES]
    out_ref[...] = rows_ref[...].astype(jnp.bfloat16)


def spectra_of(table, time_data):
    seg, mic, samples = time_data.shape
    lines = seg * mic // LANES
    return pl.pallas_call(
        spectra_kernel,
        out_shape=jax.ShapeDtypeStruct((2 * lines, LANES), jnp.bfloat16),
        in_specs=[pl.BlockSpec(memory_space=pltpu.VMEM)] * 2,
        out_specs=pl.BlockSpec(memory_space=pltpu.VMEM),
        scratch_shapes=[pltpu.VMEM((2 * lines, LANES), jnp.float32)],
        compiler_params=pltpu.CompilerParams(vmem_limit_bytes=16 * MIB),
        cost_estimate=pl.CostEstimate(
            flops=4 * time_data.size, bytes_accessed=2 * time_data.size, transcendentals=0
        ),
    )(table, time_data)


def steering_kernel(order_ref, mic_ref, grid_ref, out_ref, column, *, first_pair, samples, width):
    steer(order_ref[0], samples, own_points(grid_ref, width), mic_ref, out_ref, column, first_pair)


def steering_of(order_bin, mic_pos, grid_pos, first_pair, samples, width):
    pairs = mic_pos.shape[1] // LANES - first_pair
    return pl.pallas_call(
        functools.partial(steering_kernel, first_pair=first_pair, samples=samples, width=width),
        out_shape=jax.ShapeDtypeStruct((pairs, 2 * LANES, width), jnp.bfloat16),
        in_specs=[pl.BlockSpec(memory_space=pltpu.SMEM)] + [pl.BlockSpec(memory_space=pltpu.VMEM)] * 2,
        out_specs=pl.BlockSpec(memory_space=pltpu.VMEM),
        scratch_shapes=[pltpu.VMEM((LANES, 8), jnp.float32)],
        compiler_params=pltpu.CompilerParams(vmem_limit_bytes=16 * MIB),
        cost_estimate=pl.CostEstimate(
            flops=50 * pairs * LANES * width, bytes_accessed=4 * pairs * LANES * width, transcendentals=0
        ),
    )(order_bin, mic_pos, grid_pos)


def power_kernel(spec_ref, steer_a_ref, steer_b_ref, before_ref, out_ref, *, scale):
    groups, pairs, _, rows, _ = spec_ref.shape
    lines = rows // 2
    half = lax.broadcasted_iota(jnp.int32, (rows, LANES), 1) < LANES // 2
    beams = None
    for k in range(pairs):
        left = []
        for g in range(groups):
            lower = spec_ref[g, k, 0].astype(jnp.float32)
            upper = spec_ref[g, k, 1].astype(jnp.float32)
            even_segs = jnp.where(half, lower, pltpu.roll(upper, LANES // 2, 1))
            odd_segs = jnp.where(half, pltpu.roll(lower, LANES // 2, 1), upper)
            for x in (even_segs, odd_segs):
                turned = jnp.concatenate([-x[lines:], x[:lines]], axis=0)
                left.append(jnp.concatenate([x, turned], axis=1))
        left = jnp.concatenate(left, axis=0).astype(jnp.bfloat16)
        cut = steer_a_ref.shape[0]
        steering = steer_a_ref[k] if k < cut else steer_b_ref[k - cut]
        term = jnp.dot(left, steering, preferred_element_type=jnp.float32)
        beams = term if beams is None else beams + term
    power = jnp.sum((beams * beams).reshape(-1, 8, beams.shape[1]), axis=0) + before_ref[...]
    if scale is None:
        out_ref[...] = power
    else:
        out_ref[...] = jnp.sum(power, axis=0, keepdims=True) / jnp.float32(scale)


def power_of(spectra, steering, before, scale):
    width = steering[0].shape[2]
    size = 2 * steering[0].size
    shape = (8 if scale is None else 1, width)
    return pl.pallas_call(
        functools.partial(power_kernel, scale=scale),
        out_shape=jax.ShapeDtypeStruct(shape, jnp.float32),
        in_specs=[pl.BlockSpec(memory_space=pltpu.VMEM)] * 4,
        out_specs=pl.BlockSpec(memory_space=pltpu.VMEM),
        compiler_params=pltpu.CompilerParams(vmem_limit_bytes=16 * MIB),
        cost_estimate=pl.CostEstimate(
            flops=2 * 128 * size, bytes_accessed=2 * size, transcendentals=0
        ),
    )(spectra, *steering, before)


def shards(time_data, order_bin, mic_pos, grid_pos):
    seg_dev, mic_dev, samples = time_data.shape
    rows = lax.axis_size("row")
    seg_count = rows * lax.axis_size("core")
    mic_count = lax.axis_size("mic")
    own_width = grid_pos.shape[1] // seg_count
    denom = seg_count * seg_dev * mic_count * mic_dev * 0.375 * samples
    early = 3 * (mic_count // 2) // 4
    window, order_bin = lax.optimization_barrier((window_of(samples), order_bin))
    table, steering_a = setup_of(order_bin, window, mic_pos, grid_pos, early, own_width)
    spectra = spectra_of(table, time_data)
    every = jnp.broadcast_to(spectra[None], (rows * mic_count,) + spectra.shape)
    every = lax.all_to_all(every, ("row", "mic"), 0, 0, tiled=True)
    twin = lax.ppermute(every, "core", [(0, 1), (1, 0)])
    every, later_order = lax.optimization_barrier((every, order_bin))
    steering = (steering_a, steering_of(later_order, mic_pos, grid_pos, early, samples, own_width))
    shape = (rows, mic_count // 2, 2) + spectra.shape
    half = power_of(every.reshape(shape), steering, jnp.zeros((8, own_width), jnp.float32), None)
    return power_of(twin.reshape(shape), steering, half, denom)


def solution(mesh):
    seg_count, mic_count = mesh.shape["seg"], mesh.shape["mic"]
    split = jax.sharding.Mesh(
        mesh.devices.reshape(seg_count // 2, 2, mic_count), ("row", "core", "mic")
    )
    seg = ("row", "core")
    placed = (P(seg, "mic", None), P(), P(), P(None, "mic"))
    return jax.shard_map(
        shards, mesh=split, in_specs=placed, out_specs=P("mic", seg), check_vma=False
    )
```

time: 52.4 us -> 21.9 us (0.42)
  blocking collectives: 37.9 us -> 15.9 us
  other arithmetic: 9.86 us -> 0 us
  Pallas kernels: 0 us -> 4.3 us
  matrix products: 2.17 us -> 0 us
  local copies, waits for them, and re-layouts: 1.49 us -> 0.14 us
    all_gather x2 -> x0, blocking collectives: 37.9 us -> none  [the longest x1 31.7 us: shards(): lax.all_gather(every_segment, 'mic', axis=2, tiled=True)]
    all_to_all x0 -> x1, blocking collectives: none -> 15.9 us  [shards(): every = lax.all_to_all(every, ('row', 'mic'), 0, 0, tiled=True)]
    another operation x3 -> x0, other arithmetic: 8.18 us -> none
    pallas_call x0 -> x6, Pallas kernels: none -> 4.3 us  [the longest x2 1.3 us: power_of(): pl.pallas_call(functools.partial(power_kernel, scale=scale), out_shape=ja...]
    dot_general x2 -> x0, matrix products: 2.17 us -> none  [the longest x1 1.72 us: shards(): spec = jnp.dot(rows, table.T, preferred_element_type=jnp.float32)]
    mul x1 -> x0, other arithmetic: 1.08 us -> none  [beam_block(): (points[:, None, :] - mic_part[:, :, None]).astype(jnp.float32) * 0.001]
    unnamed x8 -> x6, local copies, waits for them, and re-layouts: 1.03 us -> 0.1 us
    div x1 -> x0, other arithmetic: 0.58 us -> none  [shards(): beam_power = jnp.sum(beams * beams, axis=0) / denom]
  transfers between devices with their start and end apart: 0 -> 1, of which waited for: 0 -> 1; matrix products, arithmetic and copies ran while one was open for 0% -> 0% of each run, Pallas kernels for 0% -> 4%
where the time goes in v3:
time: 21.9 us; the launch traced here: 21.7 us
  blocking collectives  15.9 us (73%)
  Pallas kernels  4.3 us (20%)
  between operations  0.87 us (4%)
  waiting for transfers between devices  0.47 us (2%)
    all_to_all x1, blocking collectives, shards(): every = lax.all_to_all(every, ('row', 'mic'), 0, 0, tiled=True)  15.9 us
    pallas_call x2, Pallas kernels, power_of(): pl.pallas_call(functools.partial(power_kernel, scale=scale), out_shape=ja...  1.3 us
    pallas_call x1, Pallas kernels, setup_of(): pl.pallas_call(functools.partial(setup_kernel, width=width), out_shape=[j...  1.29 us
    pallas_call x1, Pallas kernels, spectra_of(): pl.pallas_call(spectra_kernel, out_shape=jax.ShapeDtypeStruct((2 * lines,...  1.19 us
    pallas_call x1, Pallas kernels, steering_of(): pl.pallas_call(functools.partial(steering_kernel, first_pair=first_pair,...  0.5 us
    ppermute x1, waiting for transfers between devices, shards(): twin = lax.ppermute(every, 'core', [(0, 1), (1, 0)])  0.47 us
  transfers between devices with their start and end apart: 1, of which 1 were waited for; matrix products, arithmetic and copies ran while one was open for 0% of the time, Pallas kernels for 4%

profile of v3, /device:TPU:0, one launch (start us, length us, event | category | flops | bytes accessed | tf_op | source)
XLA Modules:
  0.0 21.7 jit_solution(1990999432821711320)
XLA Ops:
  0.0 0.0 copy-start.2
  0.0 0.0 copy-start.1
  0.0 0.0 copy-start
  0.8 0.0 copy-done.2
  0.9 0.0 copy-done.1
  0.9 1.3 %shard_map.47 = (bf16[8,1024]{1,0:T(8,128)(2,1)S(1)}, bf16[3,256,512]{2,1,0:T(8,128)(2,1)S(1)}) custom-call(s32[1]{0:T(128)S(6)} %copy.5.order_ref, f32[8,1024]{1,0:T(8,128)S(1)} %shard_map.46.window_ref, s32[3,512]{1,0:T(4,128)S(1)} %copy-done.2, s32[3,2048]{1,0:T(4,128)S(1)} %copy-done.1), custom_call_target="tpu_custom_call" | custom-call | flops 2147483648 | bytes 4194304 | tf_op jit(solution)/shard_map/pallas_call | solution.py:107
  2.2 0.1 copy-done
  2.2 1.2 %shard_map.48 = bf16[32,128]{1,0:T(8,128)(2,1)S(1)} custom-call(bf16[8,1024]{1,0:T(8,128)(2,1)S(1)} %get-tuple-element.13.table_ref, bf16[32,64,1024]{2,1,0:T(8,128)(2,1)S(1)} %copy-done), custom_call_target="tpu_custom_call" | custom-call | flops 8388608 | bytes 4194304 | tf_op jit(solution)/shard_map/pallas_call | solution.py:137
  3.5 15.9 %all_to_all.5 = bf16[16,32,128]{2,1,0:T(8,128)(2,1)S(1)} all-to-all(bf16[16,32,128]{2,1,0:T(8,128)(2,1)S(1)} %broadcast_in_dim.4), channel_id=1, replica_groups=mesh['row'=2,'core'=2,'mic'=8] {'row','mic'}, dimensions={0} | all-to-all | bytes 262144 | tf_op jit(solution)/shard_map/all_to_all | solution.py:224
  19.4 0.0 collective-permute-start
  19.4 0.5 %shard_map.49.steer_b_ref = bf16[1,256,512]{2,1,0:T(8,128)(2,1)S(1)} custom-call(s32[1]{0:T(128)S(6)} %copy.5.order_ref, s32[3,512]{1,0:T(4,128)S(1)} %copy-done.2, s32[3,2048]{1,0:T(4,128)S(1)} %copy-done.1), custom_call_target="tpu_custom_call" | custom-call | flops 3276800 | bytes 262144 | tf_op jit(solution)/shard_map/pallas_call | solution.py:156
  19.9 0.4 %shard_map.50.before_ref = f32[8,512]{1,0:T(8,128)S(1)} custom-call(bf16[2,4,2,32,128]{4,3,2,1,0:T(8,128)(2,1)S(1)} %bitcast.2, bf16[3,256,512]{2,1,0:T(8,128)(2,1)S(1)} %get-tuple-element.14.steer_a_ref, bf16[1,256,512]{2,1,0:T(8,128)(2,1)S(1)} %shard_map.49.steer_b_ref, f32[8,512]{1,0:T(8,128)S(1)} %broadcast_in_dim.10.before_ref), custom_call_target="tpu_custom_call" | custom-call | flops 201326592 | bytes 1572864 | tf_op jit(solution)/shard_map/pallas_call | solution.py:200
  20.3 0.5 %collective-permute-done = bf16[16,32,128]{2,1,0:T(8,128)(2,1)S(1)} collective-permute-done((bf16[16,32,128]{2,1,0:T(8,128)(2,1)S(1)}, bf16[16,32,128]{2,1,0:T(8,128)(2,1)S(1)}, u32[]{:S(2)}, u32[]{:S(2)}) %collective-permute-start) | collective-permute-done | bytes 131104 | tf_op jit(solution)/shard_map/ppermute | solution.py:225
  20.7 0.9 %shard_map.51 = f32[1,512]{1,0:T(1,128)} custom-call(bf16[2,4,2,32,128]{4,3,2,1,0:T(8,128)(2,1)S(1)} %bitcast.3, bf16[3,256,512]{2,1,0:T(8,128)(2,1)S(1)} %get-tuple-element.14.steer_a_ref, bf16[1,256,512]{2,1,0:T(8,128)(2,1)S(1)} %shard_map.49.steer_b_ref, f32[8,512]{1,0:T(8,128)S(1)} %shard_map.50.before_ref), custom_call_target="tpu_custom_call" | custom-call | flops 201326592 | bytes 1572864 | tf_op jit(solution)/shard_map/pallas_call | solution.py:200
  (3 shorter events, 0.1 us)
Async XLA Ops:
  0.0 0.8 %copy-start.2 = (s32[3,512]{1,0:T(4,128)S(1)}, s32[3,512]{1,0:T(4,128)}, u32[]{:S(2)}) copy-start(s32[3,512]{1,0:T(4,128)} %mic_ref.3) | copy-start | bytes 18436
  0.0 0.9 %copy-start.1 = (s32[3,2048]{1,0:T(4,128)S(1)}, s32[3,2048]{1,0:T(4,128)}, u32[]{:S(2)}) copy-start(s32[3,2048]{1,0:T(4,128)} %grid_ref.3) | copy-start | bytes 73732
  0.0 2.2 %copy-start = (bf16[32,64,1024]{2,1,0:T(8,128)(2,1)S(1)}, bf16[32,64,1024]{2,1,0:T(8,128)(2,1)}, u32[]{:S(2)}) copy-start(bf16[32,64,1024]{2,1,0:T(8,128)(2,1)} %data_ref.1) | copy-start | bytes 12582916
  19.4 1.3 %collective-permute-start = (bf16[16,32,128]{2,1,0:T(8,128)(2,1)S(1)}, bf16[16,32,128]{2,1,0:T(8,128)(2,1)S(1)}, u32[]{:S(2)}, u32[]{:S(2)}) collective-permute-start(bf16[16,32,128]{2,1,0:T(8,128)(2,1)S(1)} %all_to_all.5), channel_id=1, source_target_pairs={{0,8},{8,0},{1,9},{9,1},{2,10},{10,2},{3,11},{11,3},{4,12},{12,4},... | collective-permute-start | bytes 393224 | tf_op jit(solution)/shard_map/ppermute | solution.py:225

commit v4 on v3

--- a/solution.py
+++ b/solution.py
@@ -69,26 +69,23 @@
 
 def steer(order, samples, points, mic_ref, steer_ref, column, first_pair):
     per_mm = order.astype(jnp.float32) * jnp.float32(51200.0 / 343.0 / 1000.0 / samples)
+    half = LANES // 2
     for k in range(steer_ref.shape[0]):
         pair = first_pair + k
         mics = mic_ref[:, pair * LANES : (pair + 1) * LANES].astype(jnp.float32)
         mics = jnp.concatenate([mics, jnp.zeros((5, LANES), jnp.float32)], axis=0)
         column[...] = jnp.transpose(mics)
-
-        def sixteen(i, carry, k=k):
-            first = pl.multiple_of(i * 16, 16)
-            mine = column[pl.ds(first, 16), :]
+        for first in range(0, LANES, 16):
+            mine = column[first : first + 16, :]
             square = None
             for axis in range(3):
                 gap = points[axis : axis + 1, :] - mine[:, axis : axis + 1]
                 square = gap * gap if square is None else square + gap * gap
             turns = square * lax.rsqrt(jnp.maximum(square, 1.0)) * per_mm
             cosine, sine = cos_sin_turns(turns)
-            steer_ref[k, pl.ds(first, 16), :] = cosine.astype(jnp.bfloat16)
-            steer_ref[k, pl.ds(LANES + first, 16), :] = sine.astype(jnp.bfloat16)
-            return carry
-
-        lax.fori_loop(0, LANES // 16, sixteen, 0, unroll=LANES // 16)
+            row = first // half * LANES + first % half
+            steer_ref[k, row : row + 16, :] = cosine.astype(jnp.bfloat16)
+            steer_ref[k, row + half : row + half + 16, :] = (-sine).astype(jnp.bfloat16)
 
 
 def own_points(grid_ref, width):
@@ -119,16 +116,50 @@
 
 
 def spectra_kernel(table_ref, data_ref, out_ref, rows_ref):
-    seg, mic, samples = data_ref.shape
-    lines = seg * mic // LANES
-    block = data_ref[...].reshape(seg * mic, samples)
-    spec = lax.dot_general(
-        table_ref[...], block, (((1,), (1,)), ((), ())), preferred_element_type=jnp.float32
-    )
-    for line in range(lines):
-        rows_ref[pl.ds(line, 1), :] = spec[0:1, line * LANES : (line + 1) * LANES]
-        rows_ref[pl.ds(lines + line, 1), :] = spec[1:2, line * LANES : (line + 1) * LANES]
-    out_ref[...] = rows_ref[...].astype(jnp.bfloat16)
+    samples = data_ref.shape[1]
+    lines = data_ref.shape[0] // LANES
+    shares = (4, 4)
+    table = table_ref[...]
+    wide = table.astype(jnp.float32)
+    factors = [
+        [jnp.broadcast_to(wide[part : part + 1, c : c + LANES], (16, LANES)) for c in range(0, samples, LANES)]
+        for part in range(2)
+    ]
+    on_matrix = []
+    on_vector = []
+    for first in range(0, lines, sum(shares)):
+        group = min(shares[0], lines - first)
+        if group:
+            block = data_ref[pl.ds(first * LANES, group * LANES)]
+            spec = lax.dot_general(
+                table, block, (((1,), (1,)), ((), ())), preferred_element_type=jnp.float32
+            )
+            on_matrix.append((first, group, spec))
+        for line in range(first + group, min(first + sum(shares), lines)):
+            sums = ([], [])
+            for top in range(0, LANES, 16):
+                rows = data_ref[pl.ds(line * LANES + top, 16)].astype(jnp.float32)
+                for part in range(2):
+                    total = None
+                    for c, factor in enumerate(factors[part]):
+                        term = rows[:, c * LANES : (c + 1) * LANES] * factor
+                        total = term if total is None else total + term
+                    sums[part].append(total)
+            for part in range(2):
+                turned = jnp.transpose(jnp.concatenate(sums[part], axis=0))
+                on_vector.append((part * lines + line, jnp.sum(turned.reshape(-1, 8, LANES), axis=0)))
+    for first, group, spec in on_matrix:
+        for j in range(group):
+            for part in range(2):
+                rows_ref[pl.ds(part * lines + first + j, 1), :] = spec[
+                    part : part + 1, j * LANES : (j + 1) * LANES
+                ]
+    for row, eight in on_vector:
+        rows_ref[pl.ds(row, 1), :] = jnp.sum(eight, axis=0, keepdims=True)
+    real, imag = rows_ref[:lines], rows_ref[lines:]
+    half = lax.broadcasted_iota(jnp.int32, real.shape, 1) < LANES // 2
+    out_ref[:lines] = jnp.where(half, real, pltpu.roll(imag, LANES // 2, 1)).astype(jnp.bfloat16)
+    out_ref[lines:] = jnp.where(half, pltpu.roll(real, LANES // 2, 1), imag).astype(jnp.bfloat16)
 
 
 def spectra_of(table, time_data):
@@ -144,7 +175,7 @@
         cost_estimate=pl.CostEstimate(
             flops=4 * time_data.size, bytes_accessed=2 * time_data.size, transcendentals=0
         ),
-    )(table, time_data)
+    )(table, time_data.reshape(seg * mic, samples))
 
 
 def steering_kernel(order_ref, mic_ref, grid_ref, out_ref, column, *, first_pair, samples, width):
@@ -167,22 +198,18 @@
 
 
 def power_kernel(spec_ref, steer_a_ref, steer_b_ref, before_ref, out_ref, *, scale):
-    groups, pairs, _, rows, _ = spec_ref.shape
-    lines = rows // 2
-    half = lax.broadcasted_iota(jnp.int32, (rows, LANES), 1) < LANES // 2
+    groups, devices, segs, _ = spec_ref.shape
+    cut = steer_a_ref.shape[0]
+    half = lax.broadcasted_iota(jnp.int32, (segs, LANES), 1) < LANES // 2
     beams = None
-    for k in range(pairs):
-        left = []
+    for k in range(devices // 2):
+        real, imag = [], []
         for g in range(groups):
-            lower = spec_ref[g, k, 0].astype(jnp.float32)
-            upper = spec_ref[g, k, 1].astype(jnp.float32)
-            even_segs = jnp.where(half, lower, pltpu.roll(upper, LANES // 2, 1))
-            odd_segs = jnp.where(half, pltpu.roll(lower, LANES // 2, 1), upper)
-            for x in (even_segs, odd_segs):
-                turned = jnp.concatenate([-x[lines:], x[:lines]], axis=0)
-                left.append(jnp.concatenate([x, turned], axis=1))
-        left = jnp.concatenate(left, axis=0).astype(jnp.bfloat16)
-        cut = steer_a_ref.shape[0]
+            both = [spec_ref[g, 2 * k + i] for i in range(2)]
+            real.append(jnp.concatenate(both, axis=1))
+            swapped = [jnp.where(half, pltpu.roll(x, LANES // 2, 1), -pltpu.roll(x, LANES // 2, 1)) for x in both]
+            imag.append(jnp.concatenate(swapped, axis=1))
+        left = jnp.concatenate(real + imag, axis=0)
         steering = steer_a_ref[k] if k < cut else steer_b_ref[k - cut]
         term = jnp.dot(left, steering, preferred_element_type=jnp.float32)
         beams = term if beams is None else beams + term
@@ -220,12 +247,15 @@
     window, order_bin = lax.optimization_barrier((window_of(samples), order_bin))
     table, steering_a = setup_of(order_bin, window, mic_pos, grid_pos, early, own_width)
     spectra = spectra_of(table, time_data)
-    every = jnp.broadcast_to(spectra[None], (rows * mic_count,) + spectra.shape)
-    every = lax.all_to_all(every, ("row", "mic"), 0, 0, tiled=True)
+    cores = lax.axis_size("core")
+    halves = spectra.reshape(1, cores, 1, spectra.shape[0] // cores, LANES)
+    every = jnp.broadcast_to(halves, (rows, cores, mic_count) + halves.shape[3:])
+    every = every.reshape((seg_count * mic_count,) + halves.shape[3:])
+    every = lax.all_to_all(every, ("row", "core", "mic"), 0, 0, tiled=True)
     twin = lax.ppermute(every, "core", [(0, 1), (1, 0)])
     every, later_order = lax.optimization_barrier((every, order_bin))
     steering = (steering_a, steering_of(later_order, mic_pos, grid_pos, early, samples, own_width))
-    shape = (rows, mic_count // 2, 2) + spectra.shape
+    shape = (seg_count, mic_count) + halves.shape[3:]
     half = power_of(every.reshape(shape), steering, jnp.zeros((8, own_width), jnp.float32), None)
     return power_of(twin.reshape(shape), steering, half, denom)
 

time: 21.9 us -> 20.6 us (0.941)
  blocking collectives: 15.9 us -> 14.8 us
    all_to_all x1, blocking collectives: 15.9 us -> 14.8 us  [shards(): every = lax.all_to_all(every, ('row', 'core', 'mic'), 0, 0, tiled=True)]
where the time goes in v4:
time: 20.6 us; the launch traced here: 20.4 us
  blocking collectives  14.8 us (72%)
  Pallas kernels  4.15 us (20%)
  between operations  0.86 us (4%)
  waiting for transfers between devices  0.36 us (2%)
    all_to_all x1, blocking collectives, shards(): every = lax.all_to_all(every, ('row', 'core', 'mic'), 0, 0, tiled=True)  14.8 us
    pallas_call x1, Pallas kernels, setup_of(): pl.pallas_call(functools.partial(setup_kernel, width=width), out_shape=[j...  1.31 us
    pallas_call x2, Pallas kernels, power_of(): pl.pallas_call(functools.partial(power_kernel, scale=scale), out_shape=ja...  1.28 us
    pallas_call x1, Pallas kernels, spectra_of(): pl.pallas_call(spectra_kernel, out_shape=jax.ShapeDtypeStruct((2 * lines,...  1.02 us
    pallas_call x1, Pallas kernels, steering_of(): pl.pallas_call(functools.partial(steering_kernel, first_pair=first_pair,...  0.51 us
  transfers between devices with their start and end apart: 1, of which 1 were waited for; matrix products, arithmetic and copies ran while one was open for 0% of the time, Pallas kernels for 4%

profile of v4, /device:TPU:0, one launch (start us, length us, event | category | flops | bytes accessed | tf_op | source)
XLA Modules:
  0.0 20.4 jit_solution(10903341048021138169)
XLA Ops:
  0.0 0.0 copy-start.2
  0.0 0.0 copy-start.1
  0.0 0.0 copy-start
  0.8 0.0 copy-done.2
  0.9 0.0 copy-done.1
  0.9 1.3 %shard_map.47 = (bf16[8,1024]{1,0:T(8,128)(2,1)S(1)}, bf16[3,256,512]{2,1,0:T(8,128)(2,1)S(1)}) custom-call(s32[1]{0:T(128)S(6)} %copy.5.order_ref, f32[8,1024]{1,0:T(8,128)S(1)} %shard_map.46.window_ref, s32[3,512]{1,0:T(4,128)S(1)} %copy-done.2, s32[3,2048]{1,0:T(4,128)S(1)} %copy-done.1), custom_call_target="tpu_custom_call" | custom-call | flops 2147483648 | bytes 4194304 | tf_op jit(solution)/shard_map/pallas_call | solution.py:104
  2.2 0.1 copy-done
  2.2 1.0 %shard_map.48 = bf16[32,128]{1,0:T(8,128)(2,1)S(1)} custom-call(bf16[8,1024]{1,0:T(8,128)(2,1)S(1)} %get-tuple-element.13.table_ref, bf16[2048,1024]{1,0:T(8,128)(2,1)S(1)} %bitcast.5), custom_call_target="tpu_custom_call" | custom-call | flops 8388608 | bytes 4194304 | tf_op jit(solution)/shard_map/pallas_call | solution.py:168
  3.3 14.8 %all_to_all.5 = bf16[32,16,128]{2,1,0:T(8,128)(2,1)S(1)} all-to-all(bf16[32,16,128]{2,1,0:T(8,128)(2,1)S(1)} %bitcast.9), channel_id=1, replica_groups=mesh['row'=2,'core'=2,'mic'=8] {'row','core','mic'}, dimensions={0} | all-to-all | bytes 262144 | tf_op jit(solution)/shard_map/all_to_all | solution.py:254
  18.1 0.1 collective-permute-start
  18.3 0.5 %shard_map.49.steer_b_ref = bf16[1,256,512]{2,1,0:T(8,128)(2,1)S(1)} custom-call(s32[1]{0:T(128)S(6)} %copy.5.order_ref, s32[3,512]{1,0:T(4,128)S(1)} %copy-done.2, s32[3,2048]{1,0:T(4,128)S(1)} %copy-done.1), custom_call_target="tpu_custom_call" | custom-call | flops 3276800 | bytes 262144 | tf_op jit(solution)/shard_map/pallas_call | solution.py:187
  18.8 0.3 %shard_map.50.before_ref = f32[8,512]{1,0:T(8,128)S(1)} custom-call(bf16[4,8,16,128]{3,2,1,0:T(8,128)(2,1)S(1)} %bitcast.6, bf16[3,256,512]{2,1,0:T(8,128)(2,1)S(1)} %get-tuple-element.14.steer_a_ref, bf16[1,256,512]{2,1,0:T(8,128)(2,1)S(1)} %shard_map.49.steer_b_ref, f32[8,512]{1,0:T(8,128)S(1)} %broadcast_in_dim.12.before_ref), custom_call_target="tpu_custom_call" | custom-call | flops 201326592 | bytes 1572864 | tf_op jit(solution)/shard_map/pallas_call | solution.py:227
  19.1 0.4 %collective-permute-done = bf16[32,16,128]{2,1,0:T(8,128)(2,1)S(1)} collective-permute-done((bf16[32,16,128]{2,1,0:T(8,128)(2,1)S(1)}, bf16[32,16,128]{2,1,0:T(8,128)(2,1)S(1)}, u32[]{:S(2)}, u32[]{:S(2)}) %collective-permute-start) | collective-permute-done | bytes 131104 | tf_op jit(solution)/shard_map/ppermute | solution.py:255
  19.5 0.9 %shard_map.51 = f32[1,512]{1,0:T(1,128)} custom-call(bf16[4,8,16,128]{3,2,1,0:T(8,128)(2,1)S(1)} %bitcast.7, bf16[3,256,512]{2,1,0:T(8,128)(2,1)S(1)} %get-tuple-element.14.steer_a_ref, bf16[1,256,512]{2,1,0:T(8,128)(2,1)S(1)} %shard_map.49.steer_b_ref, f32[8,512]{1,0:T(8,128)S(1)} %shard_map.50.before_ref), custom_call_target="tpu_custom_call" | custom-call | flops 201326592 | bytes 1572864 | tf_op jit(solution)/shard_map/pallas_call | solution.py:227
  (3 shorter events, 0.1 us)
Async XLA Ops:
  0.0 0.8 %copy-start.2 = (s32[3,512]{1,0:T(4,128)S(1)}, s32[3,512]{1,0:T(4,128)}, u32[]{:S(2)}) copy-start(s32[3,512]{1,0:T(4,128)} %mic_ref.3) | copy-start | bytes 18436
  0.0 0.9 %copy-start.1 = (s32[3,2048]{1,0:T(4,128)S(1)}, s32[3,2048]{1,0:T(4,128)}, u32[]{:S(2)}) copy-start(s32[3,2048]{1,0:T(4,128)} %grid_ref.3) | copy-start | bytes 73732
  0.0 2.2 %copy-start = (bf16[32,64,1024]{2,1,0:T(8,128)(2,1)S(1)}, bf16[32,64,1024]{2,1,0:T(8,128)(2,1)}, u32[]{:S(2)}) copy-start(bf16[32,64,1024]{2,1,0:T(8,128)(2,1)} %param.4) | copy-start | bytes 12582916
  18.1 1.3 %collective-permute-start = (bf16[32,16,128]{2,1,0:T(8,128)(2,1)S(1)}, bf16[32,16,128]{2,1,0:T(8,128)(2,1)S(1)}, u32[]{:S(2)}, u32[]{:S(2)}) collective-permute-start(bf16[32,16,128]{2,1,0:T(8,128)(2,1)S(1)} %all_to_all.5), channel_id=1, source_target_pairs={{0,8},{8,0},{1,9},{9,1},{2,10},{10,2},{3,11},{11,3},{4,12},{12,4},... | collective-permute-start | bytes 393224 | tf_op jit(solution)/shard_map/ppermute | solution.py:255

commit v5 on v4

--- a/solution.py
+++ b/solution.py
@@ -1,5 +1,4 @@
 import functools
-import math
 
 import jax
 import jax.numpy as jnp
@@ -35,10 +34,6 @@
     r = turns - ((turns + NEAREST) - NEAREST)
     q = r * r
     return horner(COS_FIT, q), r * horner(SIN_FIT, q)
-
-
-def in_hbm(x):
-    return pltpu.with_memory_space_constraint(x, pltpu.HBM)
 
 
 def window_kernel(out_ref):
@@ -118,7 +113,7 @@
 def spectra_kernel(table_ref, data_ref, out_ref, rows_ref):
     samples = data_ref.shape[1]
     lines = data_ref.shape[0] // LANES
-    shares = (4, 4)
+    on_each = 4
     table = table_ref[...]
     wide = table.astype(jnp.float32)
     factors = [
@@ -127,15 +122,13 @@
     ]
     on_matrix = []
     on_vector = []
-    for first in range(0, lines, sum(shares)):
-        group = min(shares[0], lines - first)
-        if group:
-            block = data_ref[pl.ds(first * LANES, group * LANES)]
-            spec = lax.dot_general(
-                table, block, (((1,), (1,)), ((), ())), preferred_element_type=jnp.float32
-            )
-            on_matrix.append((first, group, spec))
-        for line in range(first + group, min(first + sum(shares), lines)):
+    for first in range(0, lines, 2 * on_each):
+        block = data_ref[pl.ds(first * LANES, on_each * LANES)]
+        spec = lax.dot_general(
+            table, block, (((1,), (1,)), ((), ())), preferred_element_type=jnp.float32
+        )
+        on_matrix.append((first, spec))
+        for line in range(first + on_each, first + 2 * on_each):
             sums = ([], [])
             for top in range(0, LANES, 16):
                 rows = data_ref[pl.ds(line * LANES + top, 16)].astype(jnp.float32)
@@ -148,8 +141,8 @@
             for part in range(2):
                 turned = jnp.transpose(jnp.concatenate(sums[part], axis=0))
                 on_vector.append((part * lines + line, jnp.sum(turned.reshape(-1, 8, LANES), axis=0)))
-    for first, group, spec in on_matrix:
-        for j in range(group):
+    for first, spec in on_matrix:
+        for j in range(on_each):
             for part in range(2):
                 rows_ref[pl.ds(part * lines + first + j, 1), :] = spec[
                     part : part + 1, j * LANES : (j + 1) * LANES
@@ -158,16 +151,21 @@
         rows_ref[pl.ds(row, 1), :] = jnp.sum(eight, axis=0, keepdims=True)
     real, imag = rows_ref[:lines], rows_ref[lines:]
     half = lax.broadcasted_iota(jnp.int32, real.shape, 1) < LANES // 2
-    out_ref[:lines] = jnp.where(half, real, pltpu.roll(imag, LANES // 2, 1)).astype(jnp.bfloat16)
-    out_ref[lines:] = jnp.where(half, pltpu.roll(real, LANES // 2, 1), imag).astype(jnp.bfloat16)
-
-
-def spectra_of(table, time_data):
+    even = jnp.where(half, real, pltpu.roll(imag, LANES // 2, 1)).astype(jnp.bfloat16)
+    odd = jnp.where(half, pltpu.roll(real, LANES // 2, 1), imag).astype(jnp.bfloat16)
+    rows, _, mics = out_ref.shape[:3]
+    for row in range(rows):
+        for mic in range(mics):
+            out_ref[row, 0, mic] = even
+            out_ref[row, 1, mic] = odd
+
+
+def spectra_of(table, time_data, devices):
     seg, mic, samples = time_data.shape
     lines = seg * mic // LANES
     return pl.pallas_call(
         spectra_kernel,
-        out_shape=jax.ShapeDtypeStruct((2 * lines, LANES), jnp.bfloat16),
+        out_shape=jax.ShapeDtypeStruct(devices + (lines, LANES), jnp.bfloat16),
         in_specs=[pl.BlockSpec(memory_space=pltpu.VMEM)] * 2,
         out_specs=pl.BlockSpec(memory_space=pltpu.VMEM),
         scratch_shapes=[pltpu.VMEM((2 * lines, LANES), jnp.float32)],
@@ -199,21 +197,25 @@
 
 def power_kernel(spec_ref, steer_a_ref, steer_b_ref, before_ref, out_ref, *, scale):
     groups, devices, segs, _ = spec_ref.shape
-    cut = steer_a_ref.shape[0]
+    width = out_ref.shape[1]
     half = lax.broadcasted_iota(jnp.int32, (segs, LANES), 1) < LANES // 2
+    real, imag = [], []
+    for g in range(groups):
+        blocks = [spec_ref[g, d] for d in range(devices)]
+        real.append(jnp.concatenate(blocks, axis=1))
+        turned = [pltpu.roll(x, LANES // 2, 1) for x in blocks]
+        imag.append(jnp.concatenate([jnp.where(half, x, -x) for x in turned], axis=1))
+    left = jnp.concatenate(real + imag, axis=0)
     beams = None
-    for k in range(devices // 2):
-        real, imag = [], []
-        for g in range(groups):
-            both = [spec_ref[g, 2 * k + i] for i in range(2)]
-            real.append(jnp.concatenate(both, axis=1))
-            swapped = [jnp.where(half, pltpu.roll(x, LANES // 2, 1), -pltpu.roll(x, LANES // 2, 1)) for x in both]
-            imag.append(jnp.concatenate(swapped, axis=1))
-        left = jnp.concatenate(real + imag, axis=0)
-        steering = steer_a_ref[k] if k < cut else steer_b_ref[k - cut]
-        term = jnp.dot(left, steering, preferred_element_type=jnp.float32)
+    start = 0
+    for ref in (steer_a_ref, steer_b_ref):
+        depth = ref.shape[0] * ref.shape[1]
+        term = jnp.dot(
+            left[:, start : start + depth], ref[...].reshape(depth, width), preferred_element_type=jnp.float32
+        )
         beams = term if beams is None else beams + term
-    power = jnp.sum((beams * beams).reshape(-1, 8, beams.shape[1]), axis=0) + before_ref[...]
+        start += depth
+    power = jnp.sum((beams * beams).reshape(-1, 8, width), axis=0) + before_ref[...]
     if scale is None:
         out_ref[...] = power
     else:
@@ -239,23 +241,21 @@
 def shards(time_data, order_bin, mic_pos, grid_pos):
     seg_dev, mic_dev, samples = time_data.shape
     rows = lax.axis_size("row")
-    seg_count = rows * lax.axis_size("core")
+    cores = lax.axis_size("core")
+    seg_count = rows * cores
     mic_count = lax.axis_size("mic")
     own_width = grid_pos.shape[1] // seg_count
     denom = seg_count * seg_dev * mic_count * mic_dev * 0.375 * samples
     early = 3 * (mic_count // 2) // 4
     window, order_bin = lax.optimization_barrier((window_of(samples), order_bin))
     table, steering_a = setup_of(order_bin, window, mic_pos, grid_pos, early, own_width)
-    spectra = spectra_of(table, time_data)
-    cores = lax.axis_size("core")
-    halves = spectra.reshape(1, cores, 1, spectra.shape[0] // cores, LANES)
-    every = jnp.broadcast_to(halves, (rows, cores, mic_count) + halves.shape[3:])
-    every = every.reshape((seg_count * mic_count,) + halves.shape[3:])
+    every = spectra_of(table, time_data, (rows, cores, mic_count))
+    every = every.reshape((seg_count * mic_count,) + every.shape[3:])
     every = lax.all_to_all(every, ("row", "core", "mic"), 0, 0, tiled=True)
     twin = lax.ppermute(every, "core", [(0, 1), (1, 0)])
     every, later_order = lax.optimization_barrier((every, order_bin))
     steering = (steering_a, steering_of(later_order, mic_pos, grid_pos, early, samples, own_width))
-    shape = (seg_count, mic_count) + halves.shape[3:]
+    shape = (seg_count, mic_count) + every.shape[1:]
     half = power_of(every.reshape(shape), steering, jnp.zeros((8, own_width), jnp.float32), None)
     return power_of(twin.reshape(shape), steering, half, denom)
 

time: 20.6 us -> 20.6 us (level)
  no operation moved by 1% of the time
where the time goes in v5:
time: 20.6 us; the launch traced here: 20.4 us
  blocking collectives  14.8 us (72%)
  Pallas kernels  4.14 us (20%)
  between operations  0.87 us (4%)
  waiting for transfers between devices  0.36 us (2%)
    all_to_all x1, blocking collectives, shards(): every = lax.all_to_all(every, ('row', 'core', 'mic'), 0, 0, tiled=True)  14.8 us
    pallas_call x1, Pallas kernels, setup_of(): pl.pallas_call(functools.partial(setup_kernel, width=width), out_shape=[j...  1.31 us
    pallas_call x2, Pallas kernels, power_of(): pl.pallas_call(functools.partial(power_kernel, scale=scale), out_shape=ja...  1.27 us
    pallas_call x1, Pallas kernels, spectra_of(): pl.pallas_call(spectra_kernel, out_shape=jax.ShapeDtypeStruct(devices + (...  1.02 us
    pallas_call x1, Pallas kernels, steering_of(): pl.pallas_call(functools.partial(steering_kernel, first_pair=first_pair,...  0.51 us
  transfers between devices with their start and end apart: 1, of which 1 were waited for; matrix products, arithmetic and copies ran while one was open for 0% of the time, Pallas kernels for 4%

profile of v5, /device:TPU:0, one launch (start us, length us, event | category | flops | bytes accessed | tf_op | source)
XLA Modules:
  0.0 20.4 jit_solution(12612791682531828558)
XLA Ops:
  0.0 0.0 copy-start.2
  0.0 0.0 copy-start.1
  0.0 0.0 copy-start
  0.8 0.0 copy-done.2
  0.9 0.0 copy-done.1
  0.9 1.3 %shard_map.47 = (bf16[8,1024]{1,0:T(8,128)(2,1)S(1)}, bf16[3,256,512]{2,1,0:T(8,128)(2,1)S(1)}) custom-call(s32[1]{0:T(128)S(6)} %copy.5.order_ref, f32[8,1024]{1,0:T(8,128)S(1)} %shard_map.46.window_ref, s32[3,512]{1,0:T(4,128)S(1)} %copy-done.2, s32[3,2048]{1,0:T(4,128)S(1)} %copy-done.1), custom_call_target="tpu_custom_call" | custom-call | flops 2147483648 | bytes 4194304 | tf_op jit(solution)/shard_map/pallas_call | solution.py:99
  2.2 0.1 copy-done
  2.2 1.0 %shard_map.48 = bf16[2,2,8,16,128]{4,3,2,1,0:T(8,128)(2,1)S(1)} custom-call(bf16[8,1024]{1,0:T(8,128)(2,1)S(1)} %get-tuple-element.13.table_ref, bf16[2048,1024]{1,0:T(8,128)(2,1)S(1)} %bitcast.4), custom_call_target="tpu_custom_call" | custom-call | flops 8388608 | bytes 4194304 | tf_op jit(solution)/shard_map/pallas_call | solution.py:166
  3.3 14.8 %all_to_all.5 = bf16[32,16,128]{2,1,0:T(8,128)(2,1)S(1)} all-to-all(bf16[32,16,128]{2,1,0:T(8,128)(2,1)S(1)} %bitcast.6), channel_id=1, replica_groups=mesh['row'=2,'core'=2,'mic'=8] {'row','core','mic'}, dimensions={0} | all-to-all | bytes 262144 | tf_op jit(solution)/shard_map/all_to_all | solution.py:254
  18.1 0.1 collective-permute-start
  18.2 0.5 %shard_map.49.steer_b_ref = bf16[1,256,512]{2,1,0:T(8,128)(2,1)S(1)} custom-call(s32[1]{0:T(128)S(6)} %copy.5.order_ref, s32[3,512]{1,0:T(4,128)S(1)} %copy-done.2, s32[3,2048]{1,0:T(4,128)S(1)} %copy-done.1), custom_call_target="tpu_custom_call" | custom-call | flops 3276800 | bytes 262144 | tf_op jit(solution)/shard_map/pallas_call | solution.py:185
  18.8 0.3 %shard_map.50.before_ref = f32[8,512]{1,0:T(8,128)S(1)} custom-call(bf16[4,8,16,128]{3,2,1,0:T(8,128)(2,1)S(1)} %bitcast.5, bf16[3,256,512]{2,1,0:T(8,128)(2,1)S(1)} %get-tuple-element.14.steer_a_ref, bf16[1,256,512]{2,1,0:T(8,128)(2,1)S(1)} %shard_map.49.steer_b_ref, f32[8,512]{1,0:T(8,128)S(1)} %broadcast_in_dim.3.before_ref), custom_call_target="tpu_custom_call" | custom-call | flops 201326592 | bytes 1572864 | tf_op jit(solution)/shard_map/pallas_call | solution.py:229
  19.1 0.4 %collective-permute-done = bf16[32,16,128]{2,1,0:T(8,128)(2,1)S(1)} collective-permute-done((bf16[32,16,128]{2,1,0:T(8,128)(2,1)S(1)}, bf16[32,16,128]{2,1,0:T(8,128)(2,1)S(1)}, u32[]{:S(2)}, u32[]{:S(2)}) %collective-permute-start) | collective-permute-done | bytes 131104 | tf_op jit(solution)/shard_map/ppermute | solution.py:255
  19.5 0.9 %shard_map.51 = f32[1,512]{1,0:T(1,128)} custom-call(bf16[4,8,16,128]{3,2,1,0:T(8,128)(2,1)S(1)} %bitcast.7, bf16[3,256,512]{2,1,0:T(8,128)(2,1)S(1)} %get-tuple-element.14.steer_a_ref, bf16[1,256,512]{2,1,0:T(8,128)(2,1)S(1)} %shard_map.49.steer_b_ref, f32[8,512]{1,0:T(8,128)S(1)} %shard_map.50.before_ref), custom_call_target="tpu_custom_call" | custom-call | flops 201326592 | bytes 1572864 | tf_op jit(solution)/shard_map/pallas_call | solution.py:229
  (2 shorter events, 0.0 us)
Async XLA Ops:
  0.0 0.8 %copy-start.2 = (s32[3,512]{1,0:T(4,128)S(1)}, s32[3,512]{1,0:T(4,128)}, u32[]{:S(2)}) copy-start(s32[3,512]{1,0:T(4,128)} %mic_ref.3) | copy-start | bytes 18436
  0.0 0.9 %copy-start.1 = (s32[3,2048]{1,0:T(4,128)S(1)}, s32[3,2048]{1,0:T(4,128)}, u32[]{:S(2)}) copy-start(s32[3,2048]{1,0:T(4,128)} %grid_ref.3) | copy-start | bytes 73732
  0.0 2.2 %copy-start = (bf16[32,64,1024]{2,1,0:T(8,128)(2,1)S(1)}, bf16[32,64,1024]{2,1,0:T(8,128)(2,1)}, u32[]{:S(2)}) copy-start(bf16[32,64,1024]{2,1,0:T(8,128)(2,1)} %param.4) | copy-start | bytes 12582916
  18.1 1.3 %collective-permute-start = (bf16[32,16,128]{2,1,0:T(8,128)(2,1)S(1)}, bf16[32,16,128]{2,1,0:T(8,128)(2,1)S(1)}, u32[]{:S(2)}, u32[]{:S(2)}) collective-permute-start(bf16[32,16,128]{2,1,0:T(8,128)(2,1)S(1)} %all_to_all.5), channel_id=1, source_target_pairs={{0,8},{8,0},{1,9},{9,1},{2,10},{10,2},{3,11},{11,3},{4,12},{12,4},... | collective-permute-start | bytes 393224 | tf_op jit(solution)/shard_map/ppermute | solution.py:255

commit v6 on v5

--- a/solution.py
+++ b/solution.py
@@ -110,46 +110,35 @@
     )(order_bin, window, mic_pos, grid_pos)
 
 
-def spectra_kernel(table_ref, data_ref, out_ref, rows_ref):
+def spectra_kernel(table_ref, data_ref, out_ref):
     samples = data_ref.shape[1]
     lines = data_ref.shape[0] // LANES
-    on_each = 4
+    shares = (4, 4)
     table = table_ref[...]
     wide = table.astype(jnp.float32)
     factors = [
-        [jnp.broadcast_to(wide[part : part + 1, c : c + LANES], (16, LANES)) for c in range(0, samples, LANES)]
+        [jnp.broadcast_to(wide[part : part + 1, c : c + LANES], (LANES, LANES)) for c in range(0, samples, LANES)]
         for part in range(2)
     ]
-    on_matrix = []
-    on_vector = []
-    for first in range(0, lines, 2 * on_each):
-        block = data_ref[pl.ds(first * LANES, on_each * LANES)]
+    pieces = ([], [])
+    for first in range(0, lines, sum(shares)):
+        block = data_ref[pl.ds(first * LANES, shares[0] * LANES)]
         spec = lax.dot_general(
             table, block, (((1,), (1,)), ((), ())), preferred_element_type=jnp.float32
         )
-        on_matrix.append((first, spec))
-        for line in range(first + on_each, first + 2 * on_each):
-            sums = ([], [])
-            for top in range(0, LANES, 16):
-                rows = data_ref[pl.ds(line * LANES + top, 16)].astype(jnp.float32)
+        for part in range(2):
+            pieces[part].extend(spec[part : part + 1, j * LANES : (j + 1) * LANES] for j in range(shares[0]))
+        for line in range(first + shares[0], first + sum(shares)):
+            sums = [None, None]
+            for c in range(samples // LANES):
+                rows = data_ref[pl.ds(line * LANES, LANES), pl.ds(c * LANES, LANES)].astype(jnp.float32)
                 for part in range(2):
-                    total = None
-                    for c, factor in enumerate(factors[part]):
-                        term = rows[:, c * LANES : (c + 1) * LANES] * factor
-                        total = term if total is None else total + term
-                    sums[part].append(total)
+                    term = rows * factors[part][c]
+                    sums[part] = term if sums[part] is None else sums[part] + term
             for part in range(2):
-                turned = jnp.transpose(jnp.concatenate(sums[part], axis=0))
-                on_vector.append((part * lines + line, jnp.sum(turned.reshape(-1, 8, LANES), axis=0)))
-    for first, spec in on_matrix:
-        for j in range(on_each):
-            for part in range(2):
-                rows_ref[pl.ds(part * lines + first + j, 1), :] = spec[
-                    part : part + 1, j * LANES : (j + 1) * LANES
-                ]
-    for row, eight in on_vector:
-        rows_ref[pl.ds(row, 1), :] = jnp.sum(eight, axis=0, keepdims=True)
-    real, imag = rows_ref[:lines], rows_ref[lines:]
+                turned = jnp.transpose(sums[part])
+                pieces[part].append(jnp.sum(turned, axis=0, keepdims=True))
+    real, imag = (jnp.concatenate(x, axis=0) for x in pieces)
     half = lax.broadcasted_iota(jnp.int32, real.shape, 1) < LANES // 2
     even = jnp.where(half, real, pltpu.roll(imag, LANES // 2, 1)).astype(jnp.bfloat16)
     odd = jnp.where(half, pltpu.roll(real, LANES // 2, 1), imag).astype(jnp.bfloat16)
@@ -168,7 +157,6 @@
         out_shape=jax.ShapeDtypeStruct(devices + (lines, LANES), jnp.bfloat16),
         in_specs=[pl.BlockSpec(memory_space=pltpu.VMEM)] * 2,
         out_specs=pl.BlockSpec(memory_space=pltpu.VMEM),
-        scratch_shapes=[pltpu.VMEM((2 * lines, LANES), jnp.float32)],
         compiler_params=pltpu.CompilerParams(vmem_limit_bytes=16 * MIB),
         cost_estimate=pl.CostEstimate(
             flops=4 * time_data.size, bytes_accessed=2 * time_data.size, transcendentals=0

time: 20.6 us -> 20.6 us (level)
  no operation moved by 1% of the time
where the time goes in v6:
time: 20.6 us; the launch traced here: 20.4 us
  blocking collectives  14.8 us (72%)
  Pallas kernels  4.13 us (20%)
  between operations  0.87 us (4%)
  waiting for transfers between devices  0.36 us (2%)
    all_to_all x1, blocking collectives, shards(): every = lax.all_to_all(every, ('row', 'core', 'mic'), 0, 0, tiled=True)  14.8 us
    pallas_call x1, Pallas kernels, setup_of(): pl.pallas_call(functools.partial(setup_kernel, width=width), out_shape=[j...  1.31 us
    pallas_call x2, Pallas kernels, power_of(): pl.pallas_call(functools.partial(power_kernel, scale=scale), out_shape=ja...  1.27 us
    pallas_call x1, Pallas kernels, spectra_of(): pl.pallas_call(spectra_kernel, out_shape=jax.ShapeDtypeStruct(devices + (...  1.01 us
    pallas_call x1, Pallas kernels, steering_of(): pl.pallas_call(functools.partial(steering_kernel, first_pair=first_pair,...  0.51 us
  transfers between devices with their start and end apart: 1, of which 1 were waited for; matrix products, arithmetic and copies ran while one was open for 0% of the time, Pallas kernels for 4%

profile of v6, /device:TPU:0, one launch (start us, length us, event | category | flops | bytes accessed | tf_op | source)
XLA Modules:
  0.0 20.4 jit_solution(8360711685238596173)
XLA Ops:
  0.0 0.0 copy-start.2
  0.0 0.0 copy-start.1
  0.0 0.0 copy-start
  0.8 0.0 copy-done.2
  0.9 0.0 copy-done.1
  0.9 1.3 %shard_map.47 = (bf16[8,1024]{1,0:T(8,128)(2,1)S(1)}, bf16[3,256,512]{2,1,0:T(8,128)(2,1)S(1)}) custom-call(s32[1]{0:T(128)S(6)} %copy.5.order_ref, f32[8,1024]{1,0:T(8,128)S(1)} %shard_map.46.window_ref, s32[3,512]{1,0:T(4,128)S(1)} %copy-done.2, s32[3,2048]{1,0:T(4,128)S(1)} %copy-done.1), custom_call_target="tpu_custom_call" | custom-call | flops 2147483648 | bytes 4194304 | tf_op jit(solution)/shard_map/pallas_call | solution.py:99
  2.2 0.1 copy-done
  2.2 1.0 %shard_map.48 = bf16[2,2,8,16,128]{4,3,2,1,0:T(8,128)(2,1)S(1)} custom-call(bf16[8,1024]{1,0:T(8,128)(2,1)S(1)} %get-tuple-element.13.table_ref, bf16[2048,1024]{1,0:T(8,128)(2,1)S(1)} %bitcast.4), custom_call_target="tpu_custom_call" | custom-call | flops 8388608 | bytes 4194304 | tf_op jit(solution)/shard_map/pallas_call | solution.py:155
  3.3 14.8 %all_to_all.5 = bf16[32,16,128]{2,1,0:T(8,128)(2,1)S(1)} all-to-all(bf16[32,16,128]{2,1,0:T(8,128)(2,1)S(1)} %bitcast.6), channel_id=1, replica_groups=mesh['row'=2,'core'=2,'mic'=8] {'row','core','mic'}, dimensions={0} | all-to-all | bytes 262144 | tf_op jit(solution)/shard_map/all_to_all | solution.py:242
  18.1 0.1 collective-permute-start
  18.2 0.5 %shard_map.49.steer_b_ref = bf16[1,256,512]{2,1,0:T(8,128)(2,1)S(1)} custom-call(s32[1]{0:T(128)S(6)} %copy.5.order_ref, s32[3,512]{1,0:T(4,128)S(1)} %copy-done.2, s32[3,2048]{1,0:T(4,128)S(1)} %copy-done.1), custom_call_target="tpu_custom_call" | custom-call | flops 3276800 | bytes 262144 | tf_op jit(solution)/shard_map/pallas_call | solution.py:173
  18.7 0.3 %shard_map.50.before_ref = f32[8,512]{1,0:T(8,128)S(1)} custom-call(bf16[4,8,16,128]{3,2,1,0:T(8,128)(2,1)S(1)} %bitcast.5, bf16[3,256,512]{2,1,0:T(8,128)(2,1)S(1)} %get-tuple-element.14.steer_a_ref, bf16[1,256,512]{2,1,0:T(8,128)(2,1)S(1)} %shard_map.49.steer_b_ref, f32[8,512]{1,0:T(8,128)S(1)} %broadcast_in_dim.3.before_ref), custom_call_target="tpu_custom_call" | custom-call | flops 201326592 | bytes 1572864 | tf_op jit(solution)/shard_map/pallas_call | solution.py:217
  19.1 0.4 %collective-permute-done = bf16[32,16,128]{2,1,0:T(8,128)(2,1)S(1)} collective-permute-done((bf16[32,16,128]{2,1,0:T(8,128)(2,1)S(1)}, bf16[32,16,128]{2,1,0:T(8,128)(2,1)S(1)}, u32[]{:S(2)}, u32[]{:S(2)}) %collective-permute-start) | collective-permute-done | bytes 131104 | tf_op jit(solution)/shard_map/ppermute | solution.py:243
  19.5 0.9 %shard_map.51 = f32[1,512]{1,0:T(1,128)} custom-call(bf16[4,8,16,128]{3,2,1,0:T(8,128)(2,1)S(1)} %bitcast.7, bf16[3,256,512]{2,1,0:T(8,128)(2,1)S(1)} %get-tuple-element.14.steer_a_ref, bf16[1,256,512]{2,1,0:T(8,128)(2,1)S(1)} %shard_map.49.steer_b_ref, f32[8,512]{1,0:T(8,128)S(1)} %shard_map.50.before_ref), custom_call_target="tpu_custom_call" | custom-call | flops 201326592 | bytes 1572864 | tf_op jit(solution)/shard_map/pallas_call | solution.py:217
  (2 shorter events, 0.0 us)
Async XLA Ops:
  0.0 0.8 %copy-start.2 = (s32[3,512]{1,0:T(4,128)S(1)}, s32[3,512]{1,0:T(4,128)}, u32[]{:S(2)}) copy-start(s32[3,512]{1,0:T(4,128)} %mic_ref.3) | copy-start | bytes 18436
  0.0 0.9 %copy-start.1 = (s32[3,2048]{1,0:T(4,128)S(1)}, s32[3,2048]{1,0:T(4,128)}, u32[]{:S(2)}) copy-start(s32[3,2048]{1,0:T(4,128)} %grid_ref.3) | copy-start | bytes 73732
  0.0 2.2 %copy-start = (bf16[32,64,1024]{2,1,0:T(8,128)(2,1)S(1)}, bf16[32,64,1024]{2,1,0:T(8,128)(2,1)}, u32[]{:S(2)}) copy-start(bf16[32,64,1024]{2,1,0:T(8,128)(2,1)} %param.4) | copy-start | bytes 12582916
  18.1 1.3 %collective-permute-start = (bf16[32,16,128]{2,1,0:T(8,128)(2,1)S(1)}, bf16[32,16,128]{2,1,0:T(8,128)(2,1)S(1)}, u32[]{:S(2)}, u32[]{:S(2)}) collective-permute-start(bf16[32,16,128]{2,1,0:T(8,128)(2,1)S(1)} %all_to_all.5), channel_id=1, source_target_pairs={{0,8},{8,0},{1,9},{9,1},{2,10},{10,2},{3,11},{11,3},{4,12},{12,4},... | collective-permute-start | bytes 393224 | tf_op jit(solution)/shard_map/ppermute | solution.py:243

commit v7 on v6

v7 whole, which is shorter than its diff:
```python
import functools

import jax
import jax.numpy as jnp
import numpy as np
from jax import lax
from jax.experimental import pallas as pl
from jax.experimental.pallas import tpu as pltpu
from jax.sharding import PartitionSpec as P

LANES = 128
MIB = 1024 * 1024


def fitted(values, degree):
    count = degree + 1
    nodes = 0.125 + 0.125 * np.cos((2 * np.arange(count) + 1) * np.pi / (2 * count))
    return [float(c) for c in np.linalg.solve(np.vander(nodes, count, increasing=True), values(nodes))]


COS_FIT = fitted(lambda q: np.cos(2 * np.pi * np.sqrt(q)), 5)
MINUS_SIN_FIT = fitted(lambda q: -np.sin(2 * np.pi * np.sqrt(q)) / np.sqrt(q), 5)


def horner(coefficients, q):
    total = q * coefficients[-1] + coefficients[-2]
    for c in coefficients[-3::-1]:
        total = total * q + c
    return total


def cos_minus_sin(turns):
    r = turns - jnp.round(turns)
    q = r * r
    return horner(COS_FIT, q), r * horner(MINUS_SIN_FIT, q)


def lead_kernel(out_ref):
    out_ref[...] = jnp.zeros(out_ref.shape, out_ref.dtype)


def lead():
    return pl.pallas_call(
        lead_kernel,
        out_shape=jax.ShapeDtypeStruct((8, LANES), jnp.float32),
        out_specs=pl.BlockSpec(memory_space=pltpu.VMEM),
        compiler_params=pltpu.CompilerParams(vmem_limit_bytes=16 * MIB),
        cost_estimate=pl.CostEstimate(flops=8 * 2**30, bytes_accessed=2**24, transcendentals=0),
    )()


def table_of(order, samples):
    times = lax.broadcasted_iota(jnp.int32, (8, samples), 1)
    row = lax.broadcasted_iota(jnp.int32, (8, samples), 0)
    turned = lax.rem(order * times, jnp.int32(samples))
    cos_w, _ = cos_minus_sin(times.astype(jnp.float32) * (1.0 / samples))
    cos_a, minus_sin_a = cos_minus_sin(turned.astype(jnp.float32) * (1.0 / samples))
    window = 0.5 - 0.5 * cos_w
    table = jnp.where(row == 0, window * cos_a, jnp.where(row == 1, window * minus_sin_a, 0.0))
    return table.astype(jnp.bfloat16)


def steer(order, samples, points, mic_ref, steer_ref, column):
    per_mm = order.astype(jnp.float32) * jnp.float32(51200.0 / 343.0 / 1000.0 / samples)
    points = points * per_mm
    half = LANES // 2
    for k in range(steer_ref.shape[0]):
        mics = mic_ref[:, k * LANES : (k + 1) * LANES].astype(jnp.float32) * per_mm
        mics = jnp.concatenate([mics, jnp.zeros((5, LANES), jnp.float32)], axis=0)
        column[...] = jnp.transpose(mics)
        for first in range(0, LANES, 16):
            mine = column[first : first + 16, :]
            square = None
            for axis in range(3):
                gap = points[axis : axis + 1, :] - mine[:, axis : axis + 1]
                square = gap * gap if square is None else square + gap * gap
            turns = square * lax.rsqrt(jnp.maximum(square, 1e-12))
            cosine, minus_sine = cos_minus_sin(turns)
            row = first // half * LANES + first % half
            steer_ref[k, row : row + 16, :] = cosine.astype(jnp.bfloat16)
            steer_ref[k, row + half : row + half + 16, :] = minus_sine.astype(jnp.bfloat16)


def own_points(grid_ref, width):
    offset = pl.multiple_of(lax.axis_index(("row", "core")) * width, width)
    return grid_ref[:, pl.ds(offset, width)].astype(jnp.float32)


def setup_kernel(order_ref, lead_ref, mic_ref, grid_ref, table_ref, steer_ref, column, *, width):
    del lead_ref
    samples = table_ref.shape[1]
    table_ref[...] = table_of(order_ref[0], samples)
    steer(order_ref[0], samples, own_points(grid_ref, width), mic_ref, steer_ref, column)


def setup_of(order_bin, first, mic_pos, grid_pos, pairs, width, samples):
    return pl.pallas_call(
        functools.partial(setup_kernel, width=width),
        out_shape=[
            jax.ShapeDtypeStruct((8, samples), jnp.bfloat16),
            jax.ShapeDtypeStruct((pairs, 2 * LANES, width), jnp.bfloat16),
        ],
        in_specs=[pl.BlockSpec(memory_space=pltpu.SMEM)] + [pl.BlockSpec(memory_space=pltpu.VMEM)] * 3,
        out_specs=[pl.BlockSpec(memory_space=pltpu.VMEM)] * 2,
        scratch_shapes=[pltpu.VMEM((LANES, 8), jnp.float32)],
        compiler_params=pltpu.CompilerParams(vmem_limit_bytes=16 * MIB),
        cost_estimate=pl.CostEstimate(flops=2 * 2**30, bytes_accessed=2**22, transcendentals=0),
    )(order_bin, first, mic_pos, grid_pos)


def spectra_kernel(table_ref, data_ref, out_ref):
    samples = data_ref.shape[1]
    lines = data_ref.shape[0] // LANES
    shares = (4, 4)
    table = table_ref[...]
    wide = table.astype(jnp.float32)
    factors = [
        [jnp.broadcast_to(wide[part : part + 1, c : c + LANES], (LANES, LANES)) for c in range(0, samples, LANES)]
        for part in range(2)
    ]
    pieces = ([], [])
    for first in range(0, lines, sum(shares)):
        block = data_ref[pl.ds(first * LANES, shares[0] * LANES)]
        spec = lax.dot_general(
            table, block, (((1,), (1,)), ((), ())), preferred_element_type=jnp.float32
        )
        for part in range(2):
            pieces[part].extend(spec[part : part + 1, j * LANES : (j + 1) * LANES] for j in range(shares[0]))
        for line in range(first + shares[0], first + sum(shares)):
            sums = [None, None]
            for c in range(samples // LANES):
                rows = data_ref[pl.ds(line * LANES, LANES), pl.ds(c * LANES, LANES)].astype(jnp.float32)
                for part in range(2):
                    term = rows * factors[part][c]
                    sums[part] = term if sums[part] is None else sums[part] + term
            for part in range(2):
                turned = jnp.transpose(sums[part])
                pieces[part].append(jnp.sum(turned, axis=0, keepdims=True))
    real, imag = (jnp.concatenate(x, axis=0) for x in pieces)
    half = lax.broadcasted_iota(jnp.int32, real.shape, 1) < LANES // 2
    even = jnp.where(half, real, pltpu.roll(imag, LANES // 2, 1)).astype(jnp.bfloat16)
    odd = jnp.where(half, pltpu.roll(real, LANES // 2, 1), imag).astype(jnp.bfloat16)
    rows, _, mics = out_ref.shape[:3]
    for row in range(rows):
        for mic in range(mics):
            out_ref[row, 0, mic] = even
            out_ref[row, 1, mic] = odd


def spectra_of(table, time_data, devices):
    seg, mic, samples = time_data.shape
    lines = seg * mic // LANES
    return pl.pallas_call(
        spectra_kernel,
        out_shape=jax.ShapeDtypeStruct(devices + (lines, LANES), jnp.bfloat16),
        in_specs=[pl.BlockSpec(memory_space=pltpu.VMEM)] * 2,
        out_specs=pl.BlockSpec(memory_space=pltpu.VMEM),
        compiler_params=pltpu.CompilerParams(vmem_limit_bytes=16 * MIB),
        cost_estimate=pl.CostEstimate(
            flops=4 * time_data.size, bytes_accessed=2 * time_data.size, transcendentals=0
        ),
    )(table, time_data.reshape(seg * mic, samples))


def power_kernel(spec_ref, steer_ref, out_ref):
    groups, devices, segs, _ = spec_ref.shape
    width = out_ref.shape[1]
    half = lax.broadcasted_iota(jnp.int32, (segs, LANES), 1) < LANES // 2
    real, imag = [], []
    for g in range(groups):
        blocks = [spec_ref[g, d] for d in range(devices)]
        real.append(jnp.concatenate(blocks, axis=1))
        turned = [pltpu.roll(x, LANES // 2, 1) for x in blocks]
        imag.append(jnp.concatenate([jnp.where(half, x, -x) for x in turned], axis=1))
    left = jnp.concatenate(real + imag, axis=0)
    steering = steer_ref[...].reshape(left.shape[1], width)
    beams = jnp.dot(left, steering, preferred_element_type=jnp.float32)
    out_ref[...] = jnp.sum(beams * beams, axis=0, keepdims=True)


def power_of(spectra, steering):
    width = steering.shape[2]
    return pl.pallas_call(
        power_kernel,
        out_shape=jax.ShapeDtypeStruct((1, width), jnp.float32),
        in_specs=[pl.BlockSpec(memory_space=pltpu.VMEM)] * 2,
        out_specs=pl.BlockSpec(memory_space=pltpu.VMEM),
        compiler_params=pltpu.CompilerParams(vmem_limit_bytes=16 * MIB),
        cost_estimate=pl.CostEstimate(
            flops=2 * 128 * steering.size, bytes_accessed=2 * steering.size, transcendentals=0
        ),
    )(spectra, steering)


def last_kernel(own_ref, other_ref, out_ref, *, scale):
    out_ref[...] = (own_ref[...] + other_ref[...]) / jnp.float32(scale)


def last_of(own, other, scale):
    return pl.pallas_call(
        functools.partial(last_kernel, scale=scale),
        out_shape=jax.ShapeDtypeStruct(own.shape, jnp.float32),
        in_specs=[pl.BlockSpec(memory_space=pltpu.VMEM)] * 2,
        out_specs=pl.BlockSpec(memory_space=pltpu.VMEM),
        compiler_params=pltpu.CompilerParams(vmem_limit_bytes=16 * MIB),
        cost_estimate=pl.CostEstimate(flops=2 * own.size, bytes_accessed=12 * own.size, transcendentals=0),
    )(own, other)


def shards(time_data, order_bin, mic_pos, grid_pos):
    seg_dev, mic_dev, samples = time_data.shape
    rows = lax.axis_size("row")
    cores = lax.axis_size("core")
    seg_count = rows * cores
    mic_count = lax.axis_size("mic")
    own_width = grid_pos.shape[1] // seg_count
    denom = seg_count * seg_dev * mic_count * mic_dev * 0.375 * samples
    swap = [(0, 1), (1, 0)]
    first, order_bin = lax.optimization_barrier((lead(), order_bin))
    table, steering = setup_of(order_bin, first, mic_pos, grid_pos, mic_count // 2, own_width, samples)
    twin_steering = lax.ppermute(steering, "core", swap)
    every = spectra_of(table, time_data, (rows, cores, mic_count))
    every = every.reshape((seg_count * mic_count,) + every.shape[3:])
    every = lax.all_to_all(every, ("row", "core", "mic"), 0, 0, tiled=True)
    every = every.reshape((seg_count, mic_count) + every.shape[1:])
    others = lax.ppermute(power_of(every, twin_steering), "core", swap)
    return last_of(power_of(every, steering), others, denom)


def solution(mesh):
    seg_count, mic_count = mesh.shape["seg"], mesh.shape["mic"]
    split = jax.sharding.Mesh(
        mesh.devices.reshape(seg_count // 2, 2, mic_count), ("row", "core", "mic")
    )
    seg = ("row", "core")
    placed = (P(seg, "mic", None), P(), P(), P(None, "mic"))
    return jax.shard_map(
        shards, mesh=split, in_specs=placed, out_specs=P("mic", seg), check_vma=False
    )
```

time: 20.6 us -> 20.7 us (level)
  starting transfers between devices: 0.11 us -> 0.7 us
  waiting for transfers between devices: 0.36 us -> 0.7 us
  Pallas kernels: 4.13 us -> 3.8 us
  blocking collectives: 14.8 us -> 14.5 us
    ppermute x1 -> x2, starting transfers between devices: 0.11 us -> 0.7 us  [the longest x1 0.53 us: shards(): twin_steering = lax.ppermute(steering, 'core', swap)]
    pallas_call x4, Pallas kernels: 1.81 us -> 1.28 us  [the longest x2 0.69 us: power_of(): pl.pallas_call(power_kernel, out_shape=jax.ShapeDtypeStruct((1, width), j...]
    all_to_all x1, blocking collectives: 14.8 us -> 14.5 us  [shards(): every = lax.all_to_all(every, ('row', 'core', 'mic'), 0, 0, tiled=True)]
    ppermute x1 -> x2, waiting for transfers between devices: 0.36 us -> 0.7 us  [the longest x1 0.7 us: shards(): others = lax.ppermute(power_of(every, twin_steering), 'core', swap)]
    pallas_call x1, Pallas kernels: 1.31 us -> 1.52 us  [setup_of(): pl.pallas_call(functools.partial(setup_kernel, width=width), out_shape=[j...]
  transfers between devices with their start and end apart: 1 -> 2, of which waited for: 1 -> 1; matrix products, arithmetic and copies ran while one was open for 0% -> 0% of each run, Pallas kernels for 4% -> 7%
where the time goes in v7:
time: 20.7 us; the launch traced here: 20.6 us
  blocking collectives  14.5 us (70%)
  Pallas kernels  3.8 us (18%)
  between operations  0.85 us (4%)
  starting transfers between devices  0.7 us (3%)
  waiting for transfers between devices  0.7 us (3%)
    all_to_all x1, blocking collectives, shards(): every = lax.all_to_all(every, ('row', 'core', 'mic'), 0, 0, tiled=True)  14.5 us
    pallas_call x1, Pallas kernels, setup_of(): pl.pallas_call(functools.partial(setup_kernel, width=width), out_shape=[j...  1.52 us
    pallas_call x1, Pallas kernels, spectra_of(): pl.pallas_call(spectra_kernel, out_shape=jax.ShapeDtypeStruct(devices + (...  1.01 us
    ppermute x1, waiting for transfers between devices, shards(): others = lax.ppermute(power_of(every, twin_steering), 'core', swap)  0.7 us
    pallas_call x2, Pallas kernels, power_of(): pl.pallas_call(power_kernel, out_shape=jax.ShapeDtypeStruct((1, width), j...  0.69 us
    pallas_call x1, Pallas kernels, last_of(): pl.pallas_call(functools.partial(last_kernel, scale=scale), out_shape=jax...  0.58 us
    ppermute x1, starting transfers between devices, shards(): twin_steering = lax.ppermute(steering, 'core', swap)  0.53 us
  transfers between devices with their start and end apart: 2, of which 1 were waited for; matrix products, arithmetic and copies ran while one was open for 0% of the time, Pallas kernels for 7%

profile of v7, /device:TPU:0, one launch (start us, length us, event | category | flops | bytes accessed | tf_op | source)
XLA Modules:
  0.0 20.6 jit_solution(4100686862271157326)
XLA Ops:
  0.0 0.0 copy-start.1
  0.0 0.0 copy-start.2
  0.0 0.0 copy-start
  0.8 0.0 copy-done.1
  0.8 0.0 copy-done.2
  0.8 1.5 %shard_map.47 = (bf16[8,1024]{1,0:T(8,128)(2,1)S(1)}, bf16[4,256,512]{2,1,0:T(8,128)(2,1)S(1)}) custom-call(s32[1]{0:T(128)S(6)} %copy.5.order_ref, f32[8,128]{1,0:T(8,128)S(1)} %shard_map.46.lead_ref, s32[3,512]{1,0:T(4,128)S(1)} %copy-done.2, s32[3,2048]{1,0:T(4,128)S(1)} %copy-done.1), custom_call_target="tpu_custom_call" | custom-call | flops 2147483648 | bytes 4194304 | tf_op jit(solution)/shard_map/pallas_call | solution.py:97
  2.4 0.5 %collective-permute-start = (bf16[4,256,512]{2,1,0:T(8,128)(2,1)S(1)}, bf16[4,256,512]{2,1,0:T(8,128)(2,1)S(1)}, u32[]{:S(2)}, u32[]{:S(2)}) collective-permute-start(bf16[4,256,512]{2,1,0:T(8,128)(2,1)S(1)} %get-tuple-element.12.steer_ref), channel_id=1, source_target_pairs={{0,8},{8,0},{1,9},{9,1},{2,10},{10,2},{3,11},{11,3},{4,12},{12,4},... | collective-permute-start | bytes 3145736 | tf_op jit(solution)/shard_map/ppermute | solution.py:221
  2.9 0.0 copy-done
  2.9 1.0 %shard_map.48 = bf16[2,2,8,16,128]{4,3,2,1,0:T(8,128)(2,1)S(1)} custom-call(bf16[8,1024]{1,0:T(8,128)(2,1)S(1)} %get-tuple-element.11.table_ref, bf16[2048,1024]{1,0:T(8,128)(2,1)S(1)} %bitcast.3), custom_call_target="tpu_custom_call" | custom-call | flops 8388608 | bytes 4194304 | tf_op jit(solution)/shard_map/pallas_call | solution.py:153
  3.9 14.5 %all_to_all.5 = bf16[32,16,128]{2,1,0:T(8,128)(2,1)S(1)} all-to-all(bf16[32,16,128]{2,1,0:T(8,128)(2,1)S(1)} %bitcast.6), channel_id=1, replica_groups=mesh['row'=2,'core'=2,'mic'=8] {'row','core','mic'}, dimensions={0} | all-to-all | bytes 262144 | tf_op jit(solution)/shard_map/all_to_all | solution.py:224
  18.4 0.0 collective-permute-done.steer_ref
  18.4 0.3 %shard_map.50 = f32[1,512]{1,0:T(1,128)S(1)} custom-call(bf16[4,8,16,128]{3,2,1,0:T(8,128)(2,1)S(1)} %bitcast.4, bf16[4,256,512]{2,1,0:T(8,128)(2,1)S(1)} %collective-permute-done.steer_ref), custom_call_target="tpu_custom_call" | custom-call | flops 134217728 | bytes 1048576 | tf_op jit(solution)/shard_map/pallas_call | solution.py:183
  18.8 0.2 collective-permute-start.1
  18.9 0.3 %shard_map.49.own_ref = f32[1,512]{1,0:T(1,128)S(1)} custom-call(bf16[4,8,16,128]{3,2,1,0:T(8,128)(2,1)S(1)} %bitcast.5, bf16[4,256,512]{2,1,0:T(8,128)(2,1)S(1)} %get-tuple-element.12.steer_ref), custom_call_target="tpu_custom_call" | custom-call | flops 134217728 | bytes 1048576 | tf_op jit(solution)/shard_map/pallas_call | solution.py:183
  19.3 0.7 %collective-permute-done.1.other_ref = f32[1,512]{1,0:T(1,128)S(1)} collective-permute-done((f32[1,512]{1,0:T(1,128)S(1)}, f32[1,512]{1,0:T(1,128)S(1)}, u32[]{:S(2)}, u32[]{:S(2)}) %collective-permute-start.1) | collective-permute-done | bytes 2080 | tf_op jit(solution)/shard_map/ppermute | solution.py:226
  20.0 0.6 %shard_map.51 = f32[1,512]{1,0:T(1,128)} custom-call(f32[1,512]{1,0:T(1,128)S(1)} %shard_map.49.own_ref, f32[1,512]{1,0:T(1,128)S(1)} %collective-permute-done.1.other_ref), custom_call_target="tpu_custom_call" | custom-call | flops 1024 | bytes 6144 | tf_op jit(solution)/shard_map/pallas_call | solution.py:200
  (1 shorter events, 0.0 us)
Async XLA Ops:
  0.0 0.8 %copy-start.1 = (s32[3,2048]{1,0:T(4,128)S(1)}, s32[3,2048]{1,0:T(4,128)}, u32[]{:S(2)}) copy-start(s32[3,2048]{1,0:T(4,128)} %grid_ref.1) | copy-start | bytes 73732
  0.0 0.8 %copy-start.2 = (s32[3,512]{1,0:T(4,128)S(1)}, s32[3,512]{1,0:T(4,128)}, u32[]{:S(2)}) copy-start(s32[3,512]{1,0:T(4,128)} %mic_ref.1) | copy-start | bytes 18436
  0.0 2.9 %copy-start = (bf16[32,64,1024]{2,1,0:T(8,128)(2,1)S(1)}, bf16[32,64,1024]{2,1,0:T(8,128)(2,1)}, u32[]{:S(2)}) copy-start(bf16[32,64,1024]{2,1,0:T(8,128)(2,1)} %param.4) | copy-start | bytes 12582916
  2.4 16.1 %collective-permute-start = (bf16[4,256,512]{2,1,0:T(8,128)(2,1)S(1)}, bf16[4,256,512]{2,1,0:T(8,128)(2,1)S(1)}, u32[]{:S(2)}, u32[]{:S(2)}) collective-permute-start(bf16[4,256,512]{2,1,0:T(8,128)(2,1)S(1)} %get-tuple-element.12.steer_ref), channel_id=1, source_target_pairs={{0,8},{8,0},{1,9},{9,1},{2,10},{10,2},{3,11},{11,3},{4,12},{12,4},... | collective-permute-start | bytes 3145736 | tf_op jit(solution)/shard_map/ppermute | solution.py:221
  18.8 1.2 %collective-permute-start.1 = (f32[1,512]{1,0:T(1,128)S(1)}, f32[1,512]{1,0:T(1,128)S(1)}, u32[]{:S(2)}, u32[]{:S(2)}) collective-permute-start(f32[1,512]{1,0:T(1,128)S(1)} %shard_map.50), channel_id=1, source_target_pairs={{0,8},{8,0},{1,9},{9,1},{2,10},{10,2},{3,11},{11,3},{4,12},{12,4},... | collective-permute-start | bytes 6152 | tf_op jit(solution)/shard_map/ppermute | solution.py:226

commit v8 on v6

--- a/solution.py
+++ b/solution.py
@@ -10,7 +10,6 @@
 
 LANES = 128
 MIB = 1024 * 1024
-NEAREST = 1.5 * 2.0**23
 
 
 def fitted(values, degree):
@@ -31,7 +30,7 @@
 
 
 def cos_sin_turns(turns):
-    r = turns - ((turns + NEAREST) - NEAREST)
+    r = turns - jnp.round(turns)
     q = r * r
     return horner(COS_FIT, q), r * horner(SIN_FIT, q)
 
@@ -64,10 +63,11 @@
 
 def steer(order, samples, points, mic_ref, steer_ref, column, first_pair):
     per_mm = order.astype(jnp.float32) * jnp.float32(51200.0 / 343.0 / 1000.0 / samples)
+    points = points * per_mm
     half = LANES // 2
     for k in range(steer_ref.shape[0]):
         pair = first_pair + k
-        mics = mic_ref[:, pair * LANES : (pair + 1) * LANES].astype(jnp.float32)
+        mics = mic_ref[:, pair * LANES : (pair + 1) * LANES].astype(jnp.float32) * per_mm
         mics = jnp.concatenate([mics, jnp.zeros((5, LANES), jnp.float32)], axis=0)
         column[...] = jnp.transpose(mics)
         for first in range(0, LANES, 16):
@@ -76,7 +76,7 @@
             for axis in range(3):
                 gap = points[axis : axis + 1, :] - mine[:, axis : axis + 1]
                 square = gap * gap if square is None else square + gap * gap
-            turns = square * lax.rsqrt(jnp.maximum(square, 1.0)) * per_mm
+            turns = square * lax.rsqrt(jnp.maximum(square, 1e-12))
             cosine, sine = cos_sin_turns(turns)
             row = first // half * LANES + first % half
             steer_ref[k, row : row + 16, :] = cosine.astype(jnp.bfloat16)
@@ -234,7 +234,7 @@
     mic_count = lax.axis_size("mic")
     own_width = grid_pos.shape[1] // seg_count
     denom = seg_count * seg_dev * mic_count * mic_dev * 0.375 * samples
-    early = 3 * (mic_count // 2) // 4
+    early = mic_count // 4
     window, order_bin = lax.optimization_barrier((window_of(samples), order_bin))
     table, steering_a = setup_of(order_bin, window, mic_pos, grid_pos, early, own_width)
     every = spectra_of(table, time_data, (rows, cores, mic_count))

time: 20.6 us -> 20.6 us (level)
  local copies, waits for them, and re-layouts: 0.08 us -> 0.49 us
  waiting for transfers between devices: 0.36 us -> 0.05 us
    pallas_call x1, Pallas kernels: 1.31 us -> 0.9 us  [setup_of(): pl.pallas_call(functools.partial(setup_kernel, width=width), out_shape=[j...]
    unnamed x6, local copies, waits for them, and re-layouts: 0.08 us -> 0.49 us
    pallas_call x1, Pallas kernels: 0.51 us -> 0.83 us  [steering_of(): pl.pallas_call(functools.partial(steering_kernel, first_pair=first_pair,...]
    ppermute x1, waiting for transfers between devices: 0.36 us -> 0.05 us  [shards(): twin = lax.ppermute(every, 'core', [(0, 1), (1, 0)])]
  transfers between devices with their start and end apart: 1 -> 1, of which waited for: 1 -> 0; matrix products, arithmetic and copies ran while one was open for 0% -> 0% of each run, Pallas kernels for 4% -> 6%
where the time goes in v8:
time: 20.6 us; the launch traced here: 20.4 us
  blocking collectives  14.8 us (72%)
  Pallas kernels  4.03 us (20%)
  between operations  0.87 us (4%)
  local copies, waits for them, and re-layouts  0.49 us (2%)
    all_to_all x1, blocking collectives, shards(): every = lax.all_to_all(every, ('row', 'core', 'mic'), 0, 0, tiled=True)  14.8 us
    pallas_call x2, Pallas kernels, power_of(): pl.pallas_call(functools.partial(power_kernel, scale=scale), out_shape=ja...  1.27 us
    pallas_call x1, Pallas kernels, spectra_of(): pl.pallas_call(spectra_kernel, out_shape=jax.ShapeDtypeStruct(devices + (...  1.01 us
    pallas_call x1, Pallas kernels, setup_of(): pl.pallas_call(functools.partial(setup_kernel, width=width), out_shape=[j...  0.9 us
    pallas_call x1, Pallas kernels, steering_of(): pl.pallas_call(functools.partial(steering_kernel, first_pair=first_pair,...  0.83 us
    unnamed x6, local copies, waits for them, and re-layouts  0.49 us
  transfers between devices with their start and end apart: 1, of which 0 were waited for; matrix products, arithmetic and copies ran while one was open for 0% of the time, Pallas kernels for 6%

profile of v8, /device:TPU:0, one launch (start us, length us, event | category | flops | bytes accessed | tf_op | source)
XLA Modules:
  0.0 20.4 jit_solution(17134843833023720502)
XLA Ops:
  0.0 0.0 copy-start.2
  0.0 0.0 copy-start.1
  0.0 0.0 copy-start
  0.8 0.0 copy-done.2
  0.9 0.0 copy-done.1
  0.9 0.9 %shard_map.47 = (bf16[8,1024]{1,0:T(8,128)(2,1)S(1)}, bf16[2,256,512]{2,1,0:T(8,128)(2,1)S(1)}) custom-call(s32[1]{0:T(128)S(6)} %copy.5.order_ref, f32[8,1024]{1,0:T(8,128)S(1)} %shard_map.46.window_ref, s32[3,512]{1,0:T(4,128)S(1)} %copy-done.2, s32[3,2048]{1,0:T(4,128)S(1)} %copy-done.1), custom_call_target="tpu_custom_call" | custom-call | flops 2147483648 | bytes 4194304 | tf_op jit(solution)/shard_map/pallas_call | solution.py:99
  1.8 0.5 %copy-done = bf16[32,64,1024]{2,1,0:T(8,128)(2,1)S(1)} copy-done((bf16[32,64,1024]{2,1,0:T(8,128)(2,1)S(1)}, bf16[32,64,1024]{2,1,0:T(8,128)(2,1)}, u32[]{:S(2)}) %copy-start) | copy-done | bytes 4194328
  2.2 1.0 %shard_map.48 = bf16[2,2,8,16,128]{4,3,2,1,0:T(8,128)(2,1)S(1)} custom-call(bf16[8,1024]{1,0:T(8,128)(2,1)S(1)} %get-tuple-element.13.table_ref, bf16[2048,1024]{1,0:T(8,128)(2,1)S(1)} %bitcast.4), custom_call_target="tpu_custom_call" | custom-call | flops 8388608 | bytes 4194304 | tf_op jit(solution)/shard_map/pallas_call | solution.py:155
  3.3 14.8 %all_to_all.5 = bf16[32,16,128]{2,1,0:T(8,128)(2,1)S(1)} all-to-all(bf16[32,16,128]{2,1,0:T(8,128)(2,1)S(1)} %bitcast.6), channel_id=1, replica_groups=mesh['row'=2,'core'=2,'mic'=8] {'row','core','mic'}, dimensions={0} | all-to-all | bytes 262144 | tf_op jit(solution)/shard_map/all_to_all | solution.py:242
  18.1 0.1 collective-permute-start
  18.2 0.8 %shard_map.49.steer_b_ref = bf16[2,256,512]{2,1,0:T(8,128)(2,1)S(1)} custom-call(s32[1]{0:T(128)S(6)} %copy.5.order_ref, s32[3,512]{1,0:T(4,128)S(1)} %copy-done.2, s32[3,2048]{1,0:T(4,128)S(1)} %copy-done.1), custom_call_target="tpu_custom_call" | custom-call | flops 6553600 | bytes 524288 | tf_op jit(solution)/shard_map/pallas_call | solution.py:173
  19.1 0.3 %shard_map.50.before_ref = f32[8,512]{1,0:T(8,128)S(1)} custom-call(bf16[4,8,16,128]{3,2,1,0:T(8,128)(2,1)S(1)} %bitcast.5, bf16[2,256,512]{2,1,0:T(8,128)(2,1)S(1)} %get-tuple-element.14.steer_a_ref, bf16[2,256,512]{2,1,0:T(8,128)(2,1)S(1)} %shard_map.49.steer_b_ref, f32[8,512]{1,0:T(8,128)S(1)} %broadcast_in_dim.3.before_ref), custom_call_target="tpu_custom_call" | custom-call | flops 134217728 | bytes 1048576 | tf_op jit(solution)/shard_map/pallas_call | solution.py:217
  19.4 0.0 collective-permute-done
  19.5 0.9 %shard_map.51 = f32[1,512]{1,0:T(1,128)} custom-call(bf16[4,8,16,128]{3,2,1,0:T(8,128)(2,1)S(1)} %bitcast.7, bf16[2,256,512]{2,1,0:T(8,128)(2,1)S(1)} %get-tuple-element.14.steer_a_ref, bf16[2,256,512]{2,1,0:T(8,128)(2,1)S(1)} %shard_map.49.steer_b_ref, f32[8,512]{1,0:T(8,128)S(1)} %shard_map.50.before_ref), custom_call_target="tpu_custom_call" | custom-call | flops 134217728 | bytes 1048576 | tf_op jit(solution)/shard_map/pallas_call | solution.py:217
  (2 shorter events, 0.0 us)
Async XLA Ops:
  0.0 0.8 %copy-start.2 = (s32[3,512]{1,0:T(4,128)S(1)}, s32[3,512]{1,0:T(4,128)}, u32[]{:S(2)}) copy-start(s32[3,512]{1,0:T(4,128)} %mic_ref.3) | copy-start | bytes 18436
  0.0 0.9 %copy-start.1 = (s32[3,2048]{1,0:T(4,128)S(1)}, s32[3,2048]{1,0:T(4,128)}, u32[]{:S(2)}) copy-start(s32[3,2048]{1,0:T(4,128)} %grid_ref.3) | copy-start | bytes 73732
  0.0 2.2 %copy-start = (bf16[32,64,1024]{2,1,0:T(8,128)(2,1)S(1)}, bf16[32,64,1024]{2,1,0:T(8,128)(2,1)}, u32[]{:S(2)}) copy-start(bf16[32,64,1024]{2,1,0:T(8,128)(2,1)} %param.4) | copy-start | bytes 12582916
  18.1 1.3 %collective-permute-start = (bf16[32,16,128]{2,1,0:T(8,128)(2,1)S(1)}, bf16[32,16,128]{2,1,0:T(8,128)(2,1)S(1)}, u32[]{:S(2)}, u32[]{:S(2)}) collective-permute-start(bf16[32,16,128]{2,1,0:T(8,128)(2,1)S(1)} %all_to_all.5), channel_id=1, source_target_pairs={{0,8},{8,0},{1,9},{9,1},{2,10},{10,2},{3,11},{11,3},{4,12},{12,4},... | collective-permute-start | bytes 393224 | tf_op jit(solution)/shard_map/ppermute | solution.py:243

commit v9 on v6

--- a/solution.py
+++ b/solution.py
@@ -88,8 +88,14 @@
     return grid_ref[:, pl.ds(offset, width)].astype(jnp.float32)
 
 
-def setup_kernel(order_ref, window_ref, mic_ref, grid_ref, table_ref, steer_ref, column, *, width):
-    table_ref[...] = table_of(order_ref[0], window_ref[...])
+def setup_kernel(
+    order_ref, window_ref, mic_ref, grid_ref, table_ref, wide_ref, steer_ref, column, *, width
+):
+    table = table_of(order_ref[0], window_ref[...])
+    table_ref[...] = table
+    for part in range(2):
+        row = table[part : part + 1].astype(jnp.float32)
+        wide_ref[part] = jnp.broadcast_to(row, wide_ref.shape[1:])
     samples = table_ref.shape[1]
     steer(order_ref[0], samples, own_points(grid_ref, width), mic_ref, steer_ref, column, 0)
 
@@ -100,26 +106,22 @@
         functools.partial(setup_kernel, width=width),
         out_shape=[
             jax.ShapeDtypeStruct((8, samples), jnp.bfloat16),
+            jax.ShapeDtypeStruct((2, 8, samples), jnp.float32),
             jax.ShapeDtypeStruct((pairs, 2 * LANES, width), jnp.bfloat16),
         ],
         in_specs=[pl.BlockSpec(memory_space=pltpu.SMEM)] + [pl.BlockSpec(memory_space=pltpu.VMEM)] * 3,
-        out_specs=[pl.BlockSpec(memory_space=pltpu.VMEM)] * 2,
+        out_specs=[pl.BlockSpec(memory_space=pltpu.VMEM)] * 3,
         scratch_shapes=[pltpu.VMEM((LANES, 8), jnp.float32)],
         compiler_params=pltpu.CompilerParams(vmem_limit_bytes=16 * MIB),
         cost_estimate=pl.CostEstimate(flops=2 * 2**30, bytes_accessed=2**22, transcendentals=0),
     )(order_bin, window, mic_pos, grid_pos)
 
 
-def spectra_kernel(table_ref, data_ref, out_ref):
+def spectra_kernel(table_ref, wide_ref, data_ref, out_ref):
     samples = data_ref.shape[1]
     lines = data_ref.shape[0] // LANES
     shares = (4, 4)
     table = table_ref[...]
-    wide = table.astype(jnp.float32)
-    factors = [
-        [jnp.broadcast_to(wide[part : part + 1, c : c + LANES], (LANES, LANES)) for c in range(0, samples, LANES)]
-        for part in range(2)
-    ]
     pieces = ([], [])
     for first in range(0, lines, sum(shares)):
         block = data_ref[pl.ds(first * LANES, shares[0] * LANES)]
@@ -132,11 +134,12 @@
             sums = [None, None]
             for c in range(samples // LANES):
                 rows = data_ref[pl.ds(line * LANES, LANES), pl.ds(c * LANES, LANES)].astype(jnp.float32)
+                rows = rows.reshape(-1, 8, LANES)
                 for part in range(2):
-                    term = rows * factors[part][c]
+                    term = rows * wide_ref[part, :, c * LANES : (c + 1) * LANES]
                     sums[part] = term if sums[part] is None else sums[part] + term
             for part in range(2):
-                turned = jnp.transpose(sums[part])
+                turned = jnp.transpose(sums[part].reshape(LANES, LANES))
                 pieces[part].append(jnp.sum(turned, axis=0, keepdims=True))
     real, imag = (jnp.concatenate(x, axis=0) for x in pieces)
     half = lax.broadcasted_iota(jnp.int32, real.shape, 1) < LANES // 2
@@ -149,19 +152,19 @@
             out_ref[row, 1, mic] = odd
 
 
-def spectra_of(table, time_data, devices):
+def spectra_of(table, wide, time_data, devices):
     seg, mic, samples = time_data.shape
     lines = seg * mic // LANES
     return pl.pallas_call(
         spectra_kernel,
         out_shape=jax.ShapeDtypeStruct(devices + (lines, LANES), jnp.bfloat16),
-        in_specs=[pl.BlockSpec(memory_space=pltpu.VMEM)] * 2,
+        in_specs=[pl.BlockSpec(memory_space=pltpu.VMEM)] * 3,
         out_specs=pl.BlockSpec(memory_space=pltpu.VMEM),
         compiler_params=pltpu.CompilerParams(vmem_limit_bytes=16 * MIB),
         cost_estimate=pl.CostEstimate(
             flops=4 * time_data.size, bytes_accessed=2 * time_data.size, transcendentals=0
         ),
-    )(table, time_data.reshape(seg * mic, samples))
+    )(table, wide, time_data.reshape(seg * mic, samples))
 
 
 def steering_kernel(order_ref, mic_ref, grid_ref, out_ref, column, *, first_pair, samples, width):
@@ -236,8 +239,8 @@
     denom = seg_count * seg_dev * mic_count * mic_dev * 0.375 * samples
     early = 3 * (mic_count // 2) // 4
     window, order_bin = lax.optimization_barrier((window_of(samples), order_bin))
-    table, steering_a = setup_of(order_bin, window, mic_pos, grid_pos, early, own_width)
-    every = spectra_of(table, time_data, (rows, cores, mic_count))
+    table, wide, steering_a = setup_of(order_bin, window, mic_pos, grid_pos, early, own_width)
+    every = spectra_of(table, wide, time_data, (rows, cores, mic_count))
     every = every.reshape((seg_count * mic_count,) + every.shape[3:])
     every = lax.all_to_all(every, ("row", "core", "mic"), 0, 0, tiled=True)
     twin = lax.ppermute(every, "core", [(0, 1), (1, 0)])

time: 20.6 us -> 20.6 us (level)
  no operation moved by 1% of the time
where the time goes in v9:
time: 20.6 us; the launch traced here: 20.4 us
  blocking collectives  14.8 us (72%)
  Pallas kernels  4.13 us (20%)
  between operations  0.87 us (4%)
  waiting for transfers between devices  0.36 us (2%)
    all_to_all x1, blocking collectives, shards(): every = lax.all_to_all(every, ('row', 'core', 'mic'), 0, 0, tiled=True)  14.8 us
    pallas_call x1, Pallas kernels, setup_of(): pl.pallas_call(functools.partial(setup_kernel, width=width), out_shape=[j...  1.32 us
    pallas_call x2, Pallas kernels, power_of(): pl.pallas_call(functools.partial(power_kernel, scale=scale), out_shape=ja...  1.27 us
    pallas_call x1, Pallas kernels, spectra_of(): pl.pallas_call(spectra_kernel, out_shape=jax.ShapeDtypeStruct(devices + (...  1.01 us
    pallas_call x1, Pallas kernels, steering_of(): pl.pallas_call(functools.partial(steering_kernel, first_pair=first_pair,...  0.51 us
  transfers between devices with their start and end apart: 1, of which 1 were waited for; matrix products, arithmetic and copies ran while one was open for 0% of the time, Pallas kernels for 4%

profile of v9, /device:TPU:0, one launch (start us, length us, event | category | flops | bytes accessed | tf_op | source)
XLA Modules:
  0.0 20.4 jit_solution(7067286444275679440)
XLA Ops:
  0.0 0.0 copy-start.2
  0.0 0.0 copy-start.1
  0.0 0.0 copy-start
  0.8 0.0 copy-done.2
  0.9 0.0 copy-done.1
  0.9 1.3 %shard_map.47 = (bf16[8,1024]{1,0:T(8,128)(2,1)S(1)}, f32[2,8,1024]{2,1,0:T(8,128)S(1)}, bf16[3,256,512]{2,1,0:T(8,128)(2,1)S(1)}) custom-call(s32[1]{0:T(128)S(6)} %copy.5.order_ref, f32[8,1024]{1,0:T(8,128)S(1)} %shard_map.46.window_ref, s32[3,512]{1,0:T(4,128)S(1)} %copy-done.2, s32[3,2048]{1,0:T(4,128)S(1)} %copy-done.1), custom_call_target="tpu_custom_call" | custom-call | flops 2147483648 | bytes 4194304 | tf_op jit(solution)/shard_map/pallas_call | solution.py:105
  2.2 0.1 copy-done
  2.2 1.0 %shard_map.48 = bf16[2,2,8,16,128]{4,3,2,1,0:T(8,128)(2,1)S(1)} custom-call(bf16[8,1024]{1,0:T(8,128)(2,1)S(1)} %get-tuple-element.14.table_ref, f32[2,8,1024]{2,1,0:T(8,128)S(1)} %get-tuple-element.15.wide_ref, bf16[2048,1024]{1,0:T(8,128)(2,1)S(1)} %bitcast.4), custom_call_target="tpu_custom_call" | custom-call | flops 8388608 | bytes 4194304 | tf_op jit(solution)/shard_map/pallas_call | solution.py:158
  3.3 14.8 %all_to_all.5 = bf16[32,16,128]{2,1,0:T(8,128)(2,1)S(1)} all-to-all(bf16[32,16,128]{2,1,0:T(8,128)(2,1)S(1)} %bitcast.6), channel_id=1, replica_groups=mesh['row'=2,'core'=2,'mic'=8] {'row','core','mic'}, dimensions={0} | all-to-all | bytes 262144 | tf_op jit(solution)/shard_map/all_to_all | solution.py:245
  18.1 0.1 collective-permute-start
  18.2 0.5 %shard_map.49.steer_b_ref = bf16[1,256,512]{2,1,0:T(8,128)(2,1)S(1)} custom-call(s32[1]{0:T(128)S(6)} %copy.5.order_ref, s32[3,512]{1,0:T(4,128)S(1)} %copy-done.2, s32[3,2048]{1,0:T(4,128)S(1)} %copy-done.1), custom_call_target="tpu_custom_call" | custom-call | flops 3276800 | bytes 262144 | tf_op jit(solution)/shard_map/pallas_call | solution.py:176
  18.7 0.3 %shard_map.50.before_ref = f32[8,512]{1,0:T(8,128)S(1)} custom-call(bf16[4,8,16,128]{3,2,1,0:T(8,128)(2,1)S(1)} %bitcast.5, bf16[3,256,512]{2,1,0:T(8,128)(2,1)S(1)} %get-tuple-element.16.steer_a_ref, bf16[1,256,512]{2,1,0:T(8,128)(2,1)S(1)} %shard_map.49.steer_b_ref, f32[8,512]{1,0:T(8,128)S(1)} %broadcast_in_dim.3.before_ref), custom_call_target="tpu_custom_call" | custom-call | flops 201326592 | bytes 1572864 | tf_op jit(solution)/shard_map/pallas_call | solution.py:220
  19.1 0.4 %collective-permute-done = bf16[32,16,128]{2,1,0:T(8,128)(2,1)S(1)} collective-permute-done((bf16[32,16,128]{2,1,0:T(8,128)(2,1)S(1)}, bf16[32,16,128]{2,1,0:T(8,128)(2,1)S(1)}, u32[]{:S(2)}, u32[]{:S(2)}) %collective-permute-start) | collective-permute-done | bytes 131104 | tf_op jit(solution)/shard_map/ppermute | solution.py:246
  19.5 0.9 %shard_map.51 = f32[1,512]{1,0:T(1,128)} custom-call(bf16[4,8,16,128]{3,2,1,0:T(8,128)(2,1)S(1)} %bitcast.7, bf16[3,256,512]{2,1,0:T(8,128)(2,1)S(1)} %get-tuple-element.16.steer_a_ref, bf16[1,256,512]{2,1,0:T(8,128)(2,1)S(1)} %shard_map.49.steer_b_ref, f32[8,512]{1,0:T(8,128)S(1)} %shard_map.50.before_ref), custom_call_target="tpu_custom_call" | custom-call | flops 201326592 | bytes 1572864 | tf_op jit(solution)/shard_map/pallas_call | solution.py:220
  (2 shorter events, 0.0 us)
Async XLA Ops:
  0.0 0.8 %copy-start.2 = (s32[3,512]{1,0:T(4,128)S(1)}, s32[3,512]{1,0:T(4,128)}, u32[]{:S(2)}) copy-start(s32[3,512]{1,0:T(4,128)} %mic_ref.3) | copy-start | bytes 18436
  0.0 0.9 %copy-start.1 = (s32[3,2048]{1,0:T(4,128)S(1)}, s32[3,2048]{1,0:T(4,128)}, u32[]{:S(2)}) copy-start(s32[3,2048]{1,0:T(4,128)} %grid_ref.3) | copy-start | bytes 73732
  0.0 2.2 %copy-start = (bf16[32,64,1024]{2,1,0:T(8,128)(2,1)S(1)}, bf16[32,64,1024]{2,1,0:T(8,128)(2,1)}, u32[]{:S(2)}) copy-start(bf16[32,64,1024]{2,1,0:T(8,128)(2,1)} %param.4) | copy-start | bytes 12582916
  18.1 1.3 %collective-permute-start = (bf16[32,16,128]{2,1,0:T(8,128)(2,1)S(1)}, bf16[32,16,128]{2,1,0:T(8,128)(2,1)S(1)}, u32[]{:S(2)}, u32[]{:S(2)}) collective-permute-start(bf16[32,16,128]{2,1,0:T(8,128)(2,1)S(1)} %all_to_all.5), channel_id=1, source_target_pairs={{0,8},{8,0},{1,9},{9,1},{2,10},{10,2},{3,11},{11,3},{4,12},{12,4},... | collective-permute-start | bytes 393224 | tf_op jit(solution)/shard_map/ppermute | solution.py:246

commit v10 on v9

--- a/solution.py
+++ b/solution.py
@@ -120,7 +120,7 @@
 def spectra_kernel(table_ref, wide_ref, data_ref, out_ref):
     samples = data_ref.shape[1]
     lines = data_ref.shape[0] // LANES
-    shares = (4, 4)
+    shares = (5, 3)
     table = table_ref[...]
     pieces = ([], [])
     for first in range(0, lines, sum(shares)):

time: 20.6 us -> 20.6 us (level)
  no operation moved by 1% of the time
where the time goes in v10:
time: 20.6 us; the launch traced here: 20.4 us
  blocking collectives  14.8 us (72%)
  Pallas kernels  4.15 us (20%)
  between operations  0.87 us (4%)
  waiting for transfers between devices  0.36 us (2%)
    all_to_all x1, blocking collectives, shards(): every = lax.all_to_all(every, ('row', 'core', 'mic'), 0, 0, tiled=True)  14.8 us
    pallas_call x1, Pallas kernels, setup_of(): pl.pallas_call(functools.partial(setup_kernel, width=width), out_shape=[j...  1.32 us
    pallas_call x2, Pallas kernels, power_of(): pl.pallas_call(functools.partial(power_kernel, scale=scale), out_shape=ja...  1.27 us
    pallas_call x1, Pallas kernels, spectra_of(): pl.pallas_call(spectra_kernel, out_shape=jax.ShapeDtypeStruct(devices + (...  1.03 us
    pallas_call x1, Pallas kernels, steering_of(): pl.pallas_call(functools.partial(steering_kernel, first_pair=first_pair,...  0.51 us
  transfers between devices with their start and end apart: 1, of which 1 were waited for; matrix products, arithmetic and copies ran while one was open for 0% of the time, Pallas kernels for 4%

profile of v10, /device:TPU:0, one launch (start us, length us, event | category | flops | bytes accessed | tf_op | source)
XLA Modules:
  0.0 20.4 jit_solution(10509249949955991275)
XLA Ops:
  0.0 0.0 copy-start.2
  0.0 0.0 copy-start.1
  0.0 0.0 copy-start
  0.8 0.0 copy-done.2
  0.9 0.0 copy-done.1
  0.9 1.3 %shard_map.47 = (bf16[8,1024]{1,0:T(8,128)(2,1)S(1)}, f32[2,8,1024]{2,1,0:T(8,128)S(1)}, bf16[3,256,512]{2,1,0:T(8,128)(2,1)S(1)}) custom-call(s32[1]{0:T(128)S(6)} %copy.5.order_ref, f32[8,1024]{1,0:T(8,128)S(1)} %shard_map.46.window_ref, s32[3,512]{1,0:T(4,128)S(1)} %copy-done.2, s32[3,2048]{1,0:T(4,128)S(1)} %copy-done.1), custom_call_target="tpu_custom_call" | custom-call | flops 2147483648 | bytes 4194304 | tf_op jit(solution)/shard_map/pallas_call | solution.py:105
  2.2 0.1 copy-done
  2.2 1.0 %shard_map.48 = bf16[2,2,8,16,128]{4,3,2,1,0:T(8,128)(2,1)S(1)} custom-call(bf16[8,1024]{1,0:T(8,128)(2,1)S(1)} %get-tuple-element.14.table_ref, f32[2,8,1024]{2,1,0:T(8,128)S(1)} %get-tuple-element.15.wide_ref, bf16[2048,1024]{1,0:T(8,128)(2,1)S(1)} %bitcast.4), custom_call_target="tpu_custom_call" | custom-call | flops 8388608 | bytes 4194304 | tf_op jit(solution)/shard_map/pallas_call | solution.py:158
  3.3 14.8 %all_to_all.5 = bf16[32,16,128]{2,1,0:T(8,128)(2,1)S(1)} all-to-all(bf16[32,16,128]{2,1,0:T(8,128)(2,1)S(1)} %bitcast.6), channel_id=1, replica_groups=mesh['row'=2,'core'=2,'mic'=8] {'row','core','mic'}, dimensions={0} | all-to-all | bytes 262144 | tf_op jit(solution)/shard_map/all_to_all | solution.py:245
  18.1 0.1 collective-permute-start
  18.2 0.5 %shard_map.49.steer_b_ref = bf16[1,256,512]{2,1,0:T(8,128)(2,1)S(1)} custom-call(s32[1]{0:T(128)S(6)} %copy.5.order_ref, s32[3,512]{1,0:T(4,128)S(1)} %copy-done.2, s32[3,2048]{1,0:T(4,128)S(1)} %copy-done.1), custom_call_target="tpu_custom_call" | custom-call | flops 3276800 | bytes 262144 | tf_op jit(solution)/shard_map/pallas_call | solution.py:176
  18.8 0.3 %shard_map.50.before_ref = f32[8,512]{1,0:T(8,128)S(1)} custom-call(bf16[4,8,16,128]{3,2,1,0:T(8,128)(2,1)S(1)} %bitcast.5, bf16[3,256,512]{2,1,0:T(8,128)(2,1)S(1)} %get-tuple-element.16.steer_a_ref, bf16[1,256,512]{2,1,0:T(8,128)(2,1)S(1)} %shard_map.49.steer_b_ref, f32[8,512]{1,0:T(8,128)S(1)} %broadcast_in_dim.3.before_ref), custom_call_target="tpu_custom_call" | custom-call | flops 201326592 | bytes 1572864 | tf_op jit(solution)/shard_map/pallas_call | solution.py:220
  19.1 0.4 %collective-permute-done = bf16[32,16,128]{2,1,0:T(8,128)(2,1)S(1)} collective-permute-done((bf16[32,16,128]{2,1,0:T(8,128)(2,1)S(1)}, bf16[32,16,128]{2,1,0:T(8,128)(2,1)S(1)}, u32[]{:S(2)}, u32[]{:S(2)}) %collective-permute-start) | collective-permute-done | bytes 131104 | tf_op jit(solution)/shard_map/ppermute | solution.py:246
  19.5 0.9 %shard_map.51 = f32[1,512]{1,0:T(1,128)} custom-call(bf16[4,8,16,128]{3,2,1,0:T(8,128)(2,1)S(1)} %bitcast.7, bf16[3,256,512]{2,1,0:T(8,128)(2,1)S(1)} %get-tuple-element.16.steer_a_ref, bf16[1,256,512]{2,1,0:T(8,128)(2,1)S(1)} %shard_map.49.steer_b_ref, f32[8,512]{1,0:T(8,128)S(1)} %shard_map.50.before_ref), custom_call_target="tpu_custom_call" | custom-call | flops 201326592 | bytes 1572864 | tf_op jit(solution)/shard_map/pallas_call | solution.py:220
  (2 shorter events, 0.0 us)
Async XLA Ops:
  0.0 0.8 %copy-start.2 = (s32[3,512]{1,0:T(4,128)S(1)}, s32[3,512]{1,0:T(4,128)}, u32[]{:S(2)}) copy-start(s32[3,512]{1,0:T(4,128)} %mic_ref.3) | copy-start | bytes 18436
  0.0 0.9 %copy-start.1 = (s32[3,2048]{1,0:T(4,128)S(1)}, s32[3,2048]{1,0:T(4,128)}, u32[]{:S(2)}) copy-start(s32[3,2048]{1,0:T(4,128)} %grid_ref.3) | copy-start | bytes 73732
  0.0 2.2 %copy-start = (bf16[32,64,1024]{2,1,0:T(8,128)(2,1)S(1)}, bf16[32,64,1024]{2,1,0:T(8,128)(2,1)}, u32[]{:S(2)}) copy-start(bf16[32,64,1024]{2,1,0:T(8,128)(2,1)} %param.4) | copy-start | bytes 12582916
  18.1 1.3 %collective-permute-start = (bf16[32,16,128]{2,1,0:T(8,128)(2,1)S(1)}, bf16[32,16,128]{2,1,0:T(8,128)(2,1)S(1)}, u32[]{:S(2)}, u32[]{:S(2)}) collective-permute-start(bf16[32,16,128]{2,1,0:T(8,128)(2,1)S(1)} %all_to_all.5), channel_id=1, source_target_pairs={{0,8},{8,0},{1,9},{9,1},{2,10},{10,2},{3,11},{11,3},{4,12},{12,4},... | collective-permute-start | bytes 393224 | tf_op jit(solution)/shard_map/ppermute | solution.py:246
